TPU v7x, 512 devices: a whole 4x8x8 slice. The times are simulated.
512 devices in a mesh: box: 128 (over z, y, x_hi), op: 4 (over x_lo, core).
Axes of the slice: x: 4 (x_hi: 2, x_lo: 2; x = x_hi * 2 + x_lo), y: 8, z: 8, core: 2. Of those that a mesh axis runs over, the one named last changes fastest.
Arguments:
- density: float32 [36864, 296], P(('box', 'op')), may hold values from -6 to 6
- operators: float32 [64, 296, 296], P('op'), may hold values from -0.046875 to 0.046875
- owner_count: int32 [128], replicated, may hold values from 96 to 288, as said below
- group_count: int32 [128], replicated, may hold values from 96 to 288, as said below
- target_slot: int32 [128, 64, 288], P('box', 'op'), may hold values from 0 to 288, as said below
- source_box: int32 [128, 64, 288], P('box', 'op'), may hold values from 0 to 24575, as said below
Outputs:
- check_potential: float32 [36864, 296], P(('box', 'op'))
Inputs may be any that keep to these rules, and one draw needn't show every extreme that they name: `owner_count`: the counts sum to 24576. The start of owner d and the start of group d (sums of earlier counts) lie within 48 of d * 192, so they differ by at most 96, and some owner holds exactly 288 boxes. `group_count`: the counts sum to 24576, starts as for owner_count; some group holds exactly 288 boxes, and in every draw some group start lies 96 above the owner start of the same index. `target_slot`: entry j of a list of group g holds j or 288; where it holds j, j is below group_count[g]. `source_box`: an entry of group g's lists lies between group_start[g] - 96 and group_start[g + 1] + 96 - 1 (group_start[128] = 24576).
All inputs are finite; a program needn't handle non-finite values.
Results may differ from a plain program's by a relative error of at most 0.0001.
Values sent between devices are 32-bit elements; how exact they have to be, the bound alone decides.
A program may use at most 64 MiB of HBM per device.

v0:
```python
import jax
import jax.numpy as jnp
from jax import lax
from jax.sharding import Mesh
from jax.sharding import PartitionSpec as P

OP = ("op_0", "op_1")
BOX_OP = ("box", "op_0", "op_1")


def shifted(block, axis, distance):
    devices = range(lax.axis_size(axis))
    route = [(i - distance, i) for i in devices if i - distance in devices]
    return lax.ppermute(block, axis, route)


def in_order(pieces, dim):
    pieces = jnp.moveaxis(pieces, 0, dim)
    lengths = pieces.shape
    return pieces.reshape(*lengths[:dim], lengths[dim] * lengths[dim + 1], *lengths[dim + 2 :])


def stacked_from(value, axes, turns):
    pieces = value
    for k in turns:
        pieces = lax.all_gather(pieces, axes[k])
    done = turns[::-1]
    back = [done.index(k) for k in range(len(axes))]
    pieces = pieces.transpose(*back, *range(len(axes), pieces.ndim))
    return pieces.reshape(-1, *value.shape)


def gathered_by_axis(value, axes, turns, dim):
    return in_order(stacked_from(value, axes, turns), dim)


def cut_along(value, dim, length):
    lengths = value.shape
    pieces = value.reshape(*lengths[:dim], length, lengths[dim] // length, *lengths[dim + 1 :])
    return jnp.moveaxis(pieces, dim, 0)


def sent_and_summed(value, axis, dim):
    pieces = cut_along(value, dim, lax.axis_size(axis))
    arrived = lax.all_to_all(pieces, axis, split_axis=0, concat_axis=0, tiled=True)
    return arrived.sum(axis=0)


def exclusive_starts(counts):
    running = jnp.cumsum(counts, dtype=jnp.int32)
    return jnp.concatenate([jnp.zeros((1,), jnp.int32), running])


def neighbours(block_rows, counts, box_index, margin):
    tail_part = lax.dynamic_slice_in_dim(block_rows, counts[box_index] - margin, margin, 0)
    from_before = shifted(tail_part, "box", 1)
    from_after = shifted(block_rows[:margin], "box", -1)
    return jnp.concatenate([from_before, block_rows, from_after], axis=0)


def window_ids(morton, starts, box_index, capacity, margin):
    this_start = starts[box_index]
    later_start = starts[box_index + 1]
    found = jnp.where(
        morton < later_start, margin + morton - this_start, margin + capacity + morton - later_start
    )
    window_len = 2 * margin + capacity
    return jnp.clip(found, 0, window_len - 1)


def relocate(block_rows, from_counts, from_starts, to_start, to_count, box_index, capacity, margin):
    window = neighbours(block_rows, from_counts, box_index, margin)
    slot_ids = jnp.arange(capacity, dtype=jnp.int32)
    found = window_ids(to_start + slot_ids, from_starts, box_index, capacity, margin)
    moved_rows = window[found]
    return jnp.where((slot_ids < to_count)[:, None], moved_rows, 0.0)


def body(density, operators, owner_count, group_count, target_slot, source_box):
    quarter = density.shape[0]
    capacity = quarter * lax.axis_size(OP)
    margin = capacity // 3
    box_index = lax.axis_index("box")
    owner_starts = exclusive_starts(owner_count)
    group_starts = exclusive_starts(group_count)
    owned_rows = gathered_by_axis(density, OP, (0, 1), 0)
    grouped = relocate(
        owned_rows,
        owner_count,
        owner_starts,
        group_starts[box_index],
        group_count[box_index],
        box_index,
        capacity,
        margin,
    )
    window = neighbours(grouped, group_count, box_index, margin)
    source_ids = window_ids(source_box[0].T, group_starts, box_index, capacity, margin)
    live_mask = (target_slot[0].T < capacity)[:, :, None]
    source_rows = jnp.where(live_mask, window[source_ids], 0.0)
    partial_value = jnp.einsum(
        "jkl,kil->ji", source_rows, operators, precision=lax.Precision.HIGHEST
    )
    column_part = sent_and_summed(partial_value, OP, 1)
    returned = relocate(
        column_part,
        group_count,
        group_starts,
        owner_starts[box_index],
        owner_count[box_index],
        box_index,
        capacity,
        margin,
    )
    return lax.all_to_all(returned, OP, split_axis=0, concat_axis=1, tiled=True)


def solution(mesh):
    torus = Mesh(mesh.devices.reshape(mesh.shape["box"], 2, 2), ("box", "op_0", "op_1"))
    placed = (P(BOX_OP, None), P(OP, None, None), P(), P(), P("box", OP, None), P("box", OP, None))
    return jax.shard_map(
        body, mesh=torus, in_specs=placed, out_specs=P(BOX_OP, None), check_vma=False
    )
```

profile of v0, /device:TPU:253, one launch (start us, length us, event | category | flops | bytes accessed | tf_op | source)
XLA Modules:
  0.0 120.2 jit_solution(3273020460535239958)
XLA Ops:
  0.0 1.2 %dynamic_slice.34 = s32[1]{0:T(128)} dynamic-slice(s32[128]{0:T(128)} %param.8, s32[]{:T(128)S(6)} %select_n.91), dynamic_slice_sizes={1} | dynamic-slice | bytes 12 | tf_op jit(solution)/shard_map/dynamic_slice | solution.py:110
  2.5 4.8 %all-gather = f32[144,296]{1,0:T(8,128)S(1)} all-gather(f32[72,296]{1,0:T(8,128)} %param.6), channel_id=2, replica_groups=mesh['box'=128,'op_0'=2,'op_1'=2] {'op_0'}, dimensions={0}, use_global_device_ids=true | all-gather | bytes 255744 | tf_op jit(solution)/shard_map/all_gather | solution.py:26
  7.4 3.3 %all-gather.1 = f32[4,72,296]{2,1,0:T(8,128)S(1)} all-gather(f32[2,72,296]{2,1,0:T(8,128)S(1)} %bitcast.34), channel_id=3, replica_groups=mesh['box'=128,'op_0'=2,'op_1'=2] {'op_1'}, dimensions={0}, use_global_device_ids=true | all-gather | bytes 511488 | tf_op jit(solution)/shard_map/all_gather | solution.py:26
  10.7 4.4 %collective-permute-start = (f32[96,296]{1,0:T(8,128)S(1)}, f32[96,296]{1,0:T(8,128)S(1)}, u32[]{:S(2)}, u32[]{:S(2)}) collective-permute-start(f32[96,296]{1,0:T(8,128)S(1)} %get-tuple-element.7), channel_id=1, source_target_pairs={{0,4},{4,8},{8,12},{12,16},{16,20},{20,24},{24,28},{28,32},{32,36}... | collective-permute-start | bytes 341000 | tf_op jit(solution)/shard_map/ppermute | solution.py:14
  15.1 2.4 %collective-permute-start.1 = (f32[96,296]{1,0:T(8,128)S(1)}, f32[96,296]{1,0:T(8,128)S(1)}, u32[]{:S(2)}, u32[]{:S(2)}) collective-permute-start(f32[96,296]{1,0:T(8,128)S(1)} %get-tuple-element.8), channel_id=1, source_target_pairs={{4,0},{8,4},{12,8},{16,12},{20,16},{24,20},{28,24},{32,28},{36,32}... | collective-permute-start | bytes 341000 | tf_op jit(solution)/shard_map/ppermute | solution.py:14
  17.5 1.3 %dynamic_slice.35 = s32[1]{0:T(128)} dynamic-slice(s32[128]{0:T(128)} %param.9, s32[]{:T(128)S(6)} %select_n.91), dynamic_slice_sizes={1} | dynamic-slice | bytes 12 | tf_op jit(solution)/shard_map/dynamic_slice | solution.py:92
  18.8 0.7 iota_compare_fusion
  20.2 0.8 copy.19
  21.0 0.2 reduce-window.18
  21.3 0.8 copy.20
  22.0 0.2 reduce-window.19
  22.4 0.6 fusion.9
  23.0 2.0 %compare_select_fusion = s32[288,16]{0,1:T(8,128)S(1)} fusion(s32[1,16,288]{2,1,0:T(8,128)} %param.11, s32[]{:T(128)} %bitcast.9, s32[]{:T(128)} %bitcast.13), kind=kLoop, calls=%fused_computation.13 | loop fusion | flops 46080 | bytes 36872 | tf_op jit(solution)/shard_map/select_n | solution.py:100
  25.7 0.7 fusion.10
  26.4 1.9 %fusion.4 = s32[288]{0:T(512)S(1)} fusion(s32[]{:T(128)} %bitcast.12, s32[]{:T(128)} %bitcast.11, s32[]{:T(128)} %bitcast.9), kind=kLoop, calls=%fused_computation.24 | loop fusion | flops 3168 | bytes 1164 | tf_op jit(solution)/shard_map/select_n | solution.py:75
  28.4 1.7 %gather_fusion = f32[288,296]{1,0:T(8,128)S(1)} fusion(f32[480,296]{1,0:T(8,128)S(1)} %pad_maximum_fusion, s32[1024]{0:T(1024)S(1)} %pad_clamp_fusion.2), kind=kCustom, calls=%fused_computation | custom fusion | bytes 683136 | tf_op jit(solution)/shard_map/gather | solution.py:75
  30.2 8.6 %collective-permute-start.2 = (f32[96,296]{1,0:T(8,128)S(1)}, f32[96,296]{1,0:T(8,128)S(1)}, u32[]{:S(2)}, u32[]{:S(2)}) collective-permute-start(f32[96,296]{1,0:T(8,128)S(1)} %get-tuple-element.5), channel_id=1, source_target_pairs={{0,4},{4,8},{8,12},{12,16},{16,20},{20,24},{24,28},{28,32},{32,36}... | collective-permute-start | bytes 341000 | tf_op jit(solution)/shard_map/ppermute | solution.py:14
  38.8 1.9 %collective-permute-start.3 = (f32[96,296]{1,0:T(8,128)S(1)}, f32[96,296]{1,0:T(8,128)S(1)}, u32[]{:S(2)}, u32[]{:S(2)}) collective-permute-start(f32[96,296]{1,0:T(8,128)S(1)} %get-tuple-element.6), channel_id=1, source_target_pairs={{4,0},{8,4},{12,8},{16,12},{20,16},{24,20},{28,24},{32,28},{36,32}... | collective-permute-start | bytes 341000 | tf_op jit(solution)/shard_map/ppermute | solution.py:14
  41.0 9.4 %collective-permute-done.3 = f32[96,296]{1,0:T(8,128)S(1)} collective-permute-done((f32[96,296]{1,0:T(8,128)S(1)}, f32[96,296]{1,0:T(8,128)S(1)}, u32[]{:S(2)}, u32[]{:S(2)}) %collective-permute-start.3) | collective-permute-done | bytes 113696 | tf_op jit(solution)/shard_map/ppermute | solution.py:14
  50.5 12.2 %gather_fusion.1 = f32[4608,296]{1,0:T(8,128)} fusion(f32[480,296]{1,0:T(8,128)S(1)} %pad_maximum_fusion.1, s32[5120]{0:T(1024)S(1)} %pad_clamp_fusion), kind=kCustom, calls=%fused_computation.1 | custom fusion | bytes 10930176 | tf_op jit(solution)/shard_map/gather | solution.py:100
  62.7 19.8 %fusion.3 = f32[288,296]{0,1:T(8,128)S(1)} fusion(f32[16,296,296]{2,1,0:T(8,128)} %param.7, f32[288,16,296]{2,1,0:T(8,128)} %bitcast.30, pred[288,16]{0,1:T(8,128)(4,1)S(1)} %compare_bitcast_fusion), kind=kOutput, calls=%fused_computation.7 | convolution fusion | flops 4846178304 | bytes 11408896 | tf_op jit(solution)/shard_map/jkl,kil->ji/dot_general | solution.py:101
  82.5 0.8 reshape.164
  83.4 5.8 %all-to-all-start = ((f32[4,288,74]{1,2,0:T(8,128)}), f32[4,288,74]{1,2,0:T(8,128)S(1)}, u32[]{:S(2)}, u32[]{:S(2)}) async-start(f32[4,288,74]{1,2,0:T(8,128)} %bitcast.19), calls=%async_computation | async-start | bytes 983040 | tf_op jit(solution)/shard_map/all_to_all | solution.py:45
  89.2 1.8 %fusion.5 = s32[288]{0:T(512)S(1)} fusion(s32[]{:T(128)} %bitcast.13, s32[]{:T(128)} %bitcast.12, s32[]{:T(128)} %bitcast.9), kind=kLoop, calls=%fused_computation.25 | loop fusion | flops 3168 | bytes 1164 | tf_op jit(solution)/shard_map/select_n | solution.py:75
  91.0 5.7 %all-to-all-done = f32[4,288,74]{1,2,0:T(8,128)S(1)} async-done(((f32[4,288,74]{1,2,0:T(8,128)}), f32[4,288,74]{1,2,0:T(8,128)S(1)}, u32[]{:S(2)}, u32[]{:S(2)}) %all-to-all-start) | async-done | bytes 341024 | tf_op jit(solution)/shard_map/all_to_all | solution.py:45
  96.9 1.9 %collective-permute-start.4 = (f32[96,74]{1,0:T(8,128)S(1)}, f32[96,74]{1,0:T(8,128)S(1)}, u32[]{:S(2)}, u32[]{:S(2)}) collective-permute-start(f32[96,74]{1,0:T(8,128)S(1)} %get-tuple-element.9), channel_id=1, source_target_pairs={{0,4},{4,8},{8,12},{12,16},{16,20},{20,24},{24,28},{28,32},{32,36}... | collective-permute-start | bytes 85256 | tf_op jit(solution)/shard_map/ppermute | solution.py:14
  98.8 4.9 %collective-permute-start.5 = (f32[96,74]{1,0:T(8,128)S(1)}, f32[96,74]{1,0:T(8,128)S(1)}, u32[]{:S(2)}, u32[]{:S(2)}) collective-permute-start(f32[96,74]{1,0:T(8,128)S(1)} %get-tuple-element.10), channel_id=1, source_target_pairs={{4,0},{8,4},{12,8},{16,12},{20,16},{24,20},{28,24},{32,28},{36,32}... | collective-permute-start | bytes 85256 | tf_op jit(solution)/shard_map/ppermute | solution.py:14
  103.7 0.7 add_compare_fusion
  104.3 5.0 %collective-permute-done.5 = f32[96,74]{1,0:T(8,128)S(1)} collective-permute-done((f32[96,74]{1,0:T(8,128)S(1)}, f32[96,74]{1,0:T(8,128)S(1)}, u32[]{:S(2)}, u32[]{:S(2)}) %collective-permute-start.5) | collective-permute-done | bytes 28448 | tf_op jit(solution)/shard_map/ppermute | solution.py:14
  109.4 1.1 gather_fusion.2
  110.6 8.8 %all_to_all.21 = f32[4,72,74]{2,1,0:T(8,128)S(1)} all-to-all(f32[4,72,74]{2,1,0:T(8,128)S(1)} %broadcast_select_fusion.1), channel_id=1, replica_groups=mesh['box'=128,'op_0'=2,'op_1'=2] {'op_0','op_1'}, dimensions={0} | all-to-all | bytes 170496 | tf_op jit(solution)/shard_map/all_to_all | solution.py:115
  119.4 0.8 all_to_all.18
  (27 shorter events, 1.1 us)
Async XLA Ops:
  0.0 40.7 %copy-start = (s32[1,16,288]{2,1,0:T(8,128)S(1)}, s32[1,16,288]{2,1,0:T(8,128)}, u32[]{:S(2)}) copy-start(s32[1,16,288]{2,1,0:T(8,128)} %param.10) | copy-start | bytes 55300
  10.7 17.6 %collective-permute-start = (f32[96,296]{1,0:T(8,128)S(1)}, f32[96,296]{1,0:T(8,128)S(1)}, u32[]{:S(2)}, u32[]{:S(2)}) collective-permute-start(f32[96,296]{1,0:T(8,128)S(1)} %get-tuple-element.7), channel_id=1, source_target_pairs={{0,4},{4,8},{8,12},{12,16},{16,20},{20,24},{24,28},{28,32},{32,36}... | collective-permute-start | bytes 341000 | tf_op jit(solution)/shard_map/ppermute | solution.py:14
  15.1 13.2 %collective-permute-start.1 = (f32[96,296]{1,0:T(8,128)S(1)}, f32[96,296]{1,0:T(8,128)S(1)}, u32[]{:S(2)}, u32[]{:S(2)}) collective-permute-start(f32[96,296]{1,0:T(8,128)S(1)} %get-tuple-element.8), channel_id=1, source_target_pairs={{4,0},{8,4},{12,8},{16,12},{20,16},{24,20},{28,24},{32,28},{36,32}... | collective-permute-start | bytes 341000 | tf_op jit(solution)/shard_map/ppermute | solution.py:14
  30.2 10.8 %collective-permute-start.2 = (f32[96,296]{1,0:T(8,128)S(1)}, f32[96,296]{1,0:T(8,128)S(1)}, u32[]{:S(2)}, u32[]{:S(2)}) collective-permute-start(f32[96,296]{1,0:T(8,128)S(1)} %get-tuple-element.5), channel_id=1, source_target_pairs={{0,4},{4,8},{8,12},{12,16},{16,20},{20,24},{24,28},{28,32},{32,36}... | collective-permute-start | bytes 341000 | tf_op jit(solution)/shard_map/ppermute | solution.py:14
  38.8 11.6 %collective-permute-start.3 = (f32[96,296]{1,0:T(8,128)S(1)}, f32[96,296]{1,0:T(8,128)S(1)}, u32[]{:S(2)}, u32[]{:S(2)}) collective-permute-start(f32[96,296]{1,0:T(8,128)S(1)} %get-tuple-element.6), channel_id=1, source_target_pairs={{4,0},{8,4},{12,8},{16,12},{20,16},{24,20},{28,24},{32,28},{36,32}... | collective-permute-start | bytes 341000 | tf_op jit(solution)/shard_map/ppermute | solution.py:14
  83.4 13.3 %all-to-all-start = ((f32[4,288,74]{1,2,0:T(8,128)}), f32[4,288,74]{1,2,0:T(8,128)S(1)}, u32[]{:S(2)}, u32[]{:S(2)}) async-start(f32[4,288,74]{1,2,0:T(8,128)} %bitcast.19), calls=%async_computation | async-start | bytes 983040 | tf_op jit(solution)/shard_map/all_to_all | solution.py:45
  96.9 7.5 %collective-permute-start.4 = (f32[96,74]{1,0:T(8,128)S(1)}, f32[96,74]{1,0:T(8,128)S(1)}, u32[]{:S(2)}, u32[]{:S(2)}) collective-permute-start(f32[96,74]{1,0:T(8,128)S(1)} %get-tuple-element.9), channel_id=1, source_target_pairs={{0,4},{4,8},{8,12},{12,16},{16,20},{20,24},{24,28},{28,32},{32,36}... | collective-permute-start | bytes 85256 | tf_op jit(solution)/shard_map/ppermute | solution.py:14
  98.8 10.6 %collective-permute-start.5 = (f32[96,74]{1,0:T(8,128)S(1)}, f32[96,74]{1,0:T(8,128)S(1)}, u32[]{:S(2)}, u32[]{:S(2)}) collective-permute-start(f32[96,74]{1,0:T(8,128)S(1)} %get-tuple-element.10), channel_id=1, source_target_pairs={{4,0},{8,4},{12,8},{16,12},{20,16},{24,20},{28,24},{32,28},{36,32}... | collective-permute-start | bytes 85256 | tf_op jit(solution)/shard_map/ppermute | solution.py:14
where the time goes:
time: 121 us; the launch traced here: 120 us
  starting transfers between devices  29.9 us (25%)
  local copies, waits for them, and re-layouts  22.4 us (19%)
  waiting for transfers between devices  20.1 us (17%)
  matrix products  19.8 us (16%)
  blocking collectives  16.9 us (14%)
  other arithmetic  8.09 us (7%)
  between operations  2.96 us (2%)
    ppermute x6, starting transfers between devices, shifted(): return lax.ppermute(block, axis, route)  24.1 us
    dot_general x1, matrix products, body(): jnp.einsum('jkl,kil->ji', source_rows, operators, precision=lax.Precision...  19.8 us
    ppermute x6, waiting for transfers between devices, shifted(): return lax.ppermute(block, axis, route)  14.4 us
    gather x1, local copies, waits for them, and re-layouts, body(): source_rows = jnp.where(live_mask, window[source_ids], 0.0)  12.2 us
    all_to_all x1, blocking collectives, body(): return lax.all_to_all(returned, OP, split_axis=0, concat_axis=1, tiled=True)  8.8 us
    all_gather x2, blocking collectives, stacked_from(): pieces = lax.all_gather(pieces, axes[k])  8.1 us
    all_to_all x1, starting transfers between devices, sent_and_summed(): lax.all_to_all(pieces, axis, split_axis=0, concat_axis=0, tiled=True)  5.79 us
    all_to_all x1, waiting for transfers between devices, sent_and_summed(): lax.all_to_all(pieces, axis, split_axis=0, concat_axis=0, tiled=True)  5.68 us
  transfers between devices with their start and end apart: 7, of which 3 were waited for; matrix products, arithmetic and copies ran while one was open for 10% of the time, Pallas kernels for 0%

commit v1 on v0

v1 whole, which is shorter than its diff:
```python
import jax
import jax.numpy as jnp
from jax import lax
from jax.experimental import pallas as pl
from jax.experimental.pallas import tpu as pltpu
from jax.sharding import PartitionSpec as P

MESH = pl.DeviceIdType.MESH
F32, BF16, I32 = jnp.float32, jnp.bfloat16, jnp.int32
ROWS = 72
CAP = 288
EDGE = 96
F = 296
HALF = 152
STEP = 144
OFFS = 16
TILES = 21
SHORT = 15
WIN = 768
KP = 1792


def iota(shape, dim):
    return lax.broadcasted_iota(I32, shape, dim)


def split(v):
    hi = v.astype(BF16)
    lo = (v - hi.astype(F32)).astype(BF16)
    return hi, lo


def slot_of_column(col):
    main = 72 * (col >> 6) + (col & 63)
    c = col & 31
    left = 72 * (c >> 3) + 64 + (c & 7)
    return jnp.where(col < 256, main, left)


def start_at(counts, index):
    lane = iota(counts.shape, 1)
    return jnp.sum(jnp.where(lane < index, counts.astype(F32), 0.0), axis=1, keepdims=True).astype(I32)


def kernel(
    den, ops, ocnt, gcnt, tgt, src, out,
    rx, stage, o_all, x_rows, xt, pmain, pleft, g_all, acc, ufold,
    hot_send, hot_recv, lpack, ra, ral, q_ref, ql_ref, ht, rq, rql, hr, tr, v_ref, fr, fin, tt,
    op_sem, ici_send, sib_send, rsem, osend, orecv,
):
    b, o = lax.axis_index("box"), lax.axis_index("op")
    n = lax.axis_size("box")
    core, chip = o % 2, o // 2
    far, sib = (o + 2) % 4, o + 1 - 2 * core
    up, down = (b + 1) % n, (b + n - 1) % n
    sibling, beside = (b, sib), (b, far)
    peers = [sibling, beside, (up, o), (up, far), (down, o), (down, far)]

    def op_copy(k, slot):
        return pltpu.make_async_copy(ops.at[k], stage.at[slot, pl.ds(0, F)], op_sem.at[slot])

    op_copy(0, 0).start()
    barrier = pltpu.get_barrier_semaphore()
    for peer in peers:
        pl.semaphore_signal(barrier, inc=1, device_id=peer, device_id_type=MESH)

    me = 4 + o
    for lt in range(3):
        parts = [den[8 * (lt + 3 * g) : 8 * (lt + 3 * g) + 8, 256:F] for g in range(3)]
        rx[me, lt] = jnp.concatenate([*parts, jnp.zeros((8, 8), F32)], axis=1)
    for rt in range(9):
        for h in range(2):
            rx[me, 3 + 2 * rt + h] = den[8 * rt : 8 * rt + 8, 128 * h : 128 * h + 128]

    def block_copy(here, there, count, send, device):
        return pltpu.make_async_remote_copy(
            src_ref=rx.at[here, pl.ds(0, count)], dst_ref=rx.at[there, pl.ds(0, count)],
            send_sem=send, recv_sem=rsem.at[there], device_id=device, device_id_type=MESH,
        )

    pl.semaphore_wait(barrier, len(peers))

    def to_prev_segment(i):
        return block_copy(me, o, TILES, ici_send.at[1 + i], peers[2 + i])

    def to_next_segment(i, count):
        return block_copy(me, 8 + o, count, ici_send.at[3 + i], peers[4 + i])

    to_beside = block_copy(me, me, TILES, ici_send.at[0], beside)
    to_sibling = block_copy(me, me, TILES, sib_send.at[0], sibling)
    for i in (1, 0):
        to_prev_segment(i).start()

        @pl.when(o < 2)
        def _():
            to_next_segment(i, TILES).start()

        @pl.when(o == 2)
        def _():
            to_next_segment(i, SHORT).start()

    to_beside.start()
    to_sibling.start()

    counts_o, counts_g = ocnt[...], gcnt[...]
    os0, os1, os2 = (start_at(counts_o, b + i) for i in (-1, 0, 1))
    gs1, gs2 = (start_at(counts_g, b + i) for i in (0, 1))
    shift = gs1 - os1
    m = src[0]
    place = jnp.where(m < os1, m - os0, jnp.where(m < os2, CAP + m - os1, 2 * CAP + m - os2))
    place = jnp.where(tgt[0] < CAP, place, -1)
    j = iota((CAP, 384), 0) + shift
    j = jnp.where(j < 0, j + CAP, jnp.where(j >= CAP, j - CAP, j))
    turn = jnp.where(j == slot_of_column(iota((CAP, 384), 1)), 1.0, 0.0).astype(F32)
    turned = jnp.dot(place.astype(F32), turn, precision=lax.Precision.HIGHEST, preferred_element_type=F32)
    turned = (turned + 0.25 * jnp.where(turned < 0, -1.0, 1.0)).astype(I32)
    pmain[...] = turned[:, :256]
    group_of_lane = iota((1, 128), 1) >> 5
    for t in range(2):
        rows = []
        for h in range(2):
            row = jnp.zeros((1, 128), I32)
            for a in range(4):
                k = 8 * t + 4 * h + a
                row = jnp.where(group_of_lane == a, turned[k : k + 1, 256:384], row)
            rows.append(row)
        pleft[t : t + 1] = jnp.concatenate(rows, axis=1)

    s = slot_of_column(iota((384, 128), 0))
    real = iota((384, 128), 0) < CAP
    lane = iota((384, 128), 1)
    is_head = real & (s >= CAP - EDGE) & (os1 + s - CAP >= gs1) & (s - (CAP - EDGE) == lane)
    box1 = os1 + s
    tail = jnp.where((box1 >= os2) & (box1 < gs2), box1 - os2, jnp.where(box1 + CAP < gs2, box1 + CAP - os2, -1))
    hot_send[:, :128] = jnp.where(is_head, 1.0, 0.0).astype(BF16)
    hot_send[:, 128:] = jnp.where(real & (tail == lane), 1.0, 0.0).astype(BF16)
    r = iota((256, 128), 0)
    slot = jnp.where(r < 128, os2 - os1 + r - EDGE, r - 128)
    known = jnp.where(r < 128, r, r - 128) < EDGE
    lane = iota((256, 128), 1)
    hot_recv[:, :128] = jnp.where(known & (slot == slot_of_column(lane + 128 * chip)), 1.0, 0.0).astype(BF16)
    hot_recv[:, 128:] = jnp.where(known & (lane < 32) & (slot == slot_of_column(lane + 256)), 1.0, 0.0).astype(BF16)

    stage[:, pl.ds(F, 8), :] = jnp.zeros((2, 8, F), F32)

    def split_pair(q, _):
        for par in range(2):
            k = 2 * q + par

            @pl.when(k < OFFS - 1)
            def _():
                op_copy(k + 1, 1 - par).start()

            op_copy(k, par).wait()
            v = stage[par]
            hi = v.astype(BF16)
            hi32 = hi.astype(F32)
            lo32 = v - hi32
            base = 768 * par
            o_all[q, :, base : base + 256] = hi[:, :256]
            o_all[q, :, base + 256 : base + 512] = hi[:, :256]
            o_all[q, :, base + 512 : base + 768] = lo32[:, :256].astype(BF16)
            last = jnp.concatenate([hi32[:, 256:], hi32[:, 256:], lo32[:, 256:], jnp.zeros((304, 8), F32)], axis=1)
            o_all[q, :, 1536 + 128 * par : 1664 + 128 * par] = last.astype(BF16)
        return 0

    lax.fori_loop(0, OFFS // 2, split_pair, 0)

    def arrived(there, count=TILES):
        block_copy(there, there, count, ici_send.at[0], sibling).wait_recv()

    def hand_on(i, there, count=TILES):
        return block_copy(there, there, count, sib_send.at[i], sibling)

    passed = [4 + far, o, far, 8 + core]
    for i, there in enumerate(passed):
        arrived(there)
        hand_on(1 + i, there).start()

    @pl.when(core == 0)
    def _():
        arrived(10, SHORT)
        hand_on(5, 10, SHORT).start()

    for there in (4 + sib, 4 + (sib + 2) % 4, sib, (sib + 2) % 4, 8 + 1 - core):
        arrived(there)

    @pl.when(core == 1)
    def _():
        arrived(10, SHORT)

    def unpack(idx, rts):
        base = pl.multiple_of(ROWS * idx, 8)
        for rt in rts:
            at = pl.ds(base + 8 * rt, 8)
            for h in range(2):
                x_rows[at, 128 * h : 128 * h + 128] = rx[idx, 3 + 2 * rt + h]
            g = rt // 3
            left = rx[idx, rt % 3]
            x_rows[at, 256:384] = pltpu.roll(left, 128 - 40 * g, 1) if g else left

    def unpack_full(idx, _):
        unpack(idx, range(9))
        return 0

    lax.fori_loop(0, 10, unpack_full, 0)
    unpack(10, range(6))

    for i in range(WIN // 128):
        t = x_rows[128 * i : 128 * i + 128, :].T
        hi32 = t.astype(BF16).astype(F32)
        lo32 = t - hi32
        xt[:, 128 * i : 128 * i + 128] = jnp.concatenate(
            [hi32[:256], lo32[:256], hi32[256:F], lo32[256:F]], axis=0
        ).astype(BF16)

    def gathered(row):
        hot = jnp.where(iota((WIN, 256), 0) == row, 1.0, 0.0).astype(BF16)
        return jnp.dot(xt[...], hot, preferred_element_type=F32)

    def last_rows(g):
        return jnp.concatenate([g[512:592], g[512:552], jnp.zeros((8, g.shape[1]), F32)], axis=0).astype(BF16)

    def gather_pair(q, _):
        for par in range(2):
            g = gathered(pmain[pl.ds(2 * q + par, 1), :])
            hi, lo = g[:256].astype(BF16), g[256:512].astype(BF16)
            base = 768 * par
            g_all[q, base : base + 256, :256] = hi
            g_all[q, base + 256 : base + 512, :256] = lo
            g_all[q, base + 512 : base + 768, :256] = hi
            g_all[q, 1536 + 128 * par : 1664 + 128 * par, :256] = last_rows(g)
        return 0

    lax.fori_loop(0, OFFS // 2, gather_pair, 0)

    def gather_left(t, _):
        g = gathered(pleft[pl.ds(t, 1), :])
        for kk in range(8):
            h, a = kk // 4, kk % 4
            part = jnp.where(group_of_lane == a, g[:, 128 * h : 128 * h + 128], 0.0)
            hi, lo = part[:256].astype(BF16), part[256:512].astype(BF16)
            q, base = 4 * t + kk // 2, 768 * (kk % 2)
            g_all[q, base : base + 256, 256:] = hi
            g_all[q, base + 256 : base + 512, 256:] = lo
            g_all[q, base + 512 : base + 768, 256:] = hi
            g_all[q, 1536 + 128 * (kk % 2) : 1664 + 128 * (kk % 2), 256:] = last_rows(part)
        return 0

    lax.fori_loop(0, 2, gather_left, 0)

    acc[...] = jnp.dot(o_all[0], g_all[0], preferred_element_type=F32)

    def multiply(q, _):
        acc[...] += jnp.dot(o_all[q], g_all[q], preferred_element_type=F32)
        return 0

    lax.fori_loop(1, OFFS // 2, multiply, 0)

    u = acc[:, 256:384]
    u = u + pltpu.roll(u, 64, 1)
    ufold[...] = u + pltpu.roll(u, 32, 1)

    def packed(half):
        v = ufold[pl.ds(pl.multiple_of(STEP * half, 8), 160), :]
        row = jnp.zeros((40, 128), F32)
        for a in range(4):
            row = jnp.where(group_of_lane == a, v[40 * a : 40 * a + 40], row)
        return row

    def unpacked(v):
        parts = [v if a == 0 else pltpu.roll(v, 128 - 32 * a, 1) for a in range(4)]
        return jnp.concatenate(parts, axis=0)[:HALF]

    def send(i, source, target, device, recv=None):
        return pltpu.make_async_remote_copy(
            src_ref=source, dst_ref=target, send_sem=osend.at[i], recv_sem=orecv.at[i if recv is None else recv],
            device_id=device, device_id_type=MESH,
        )

    theirs = pl.ds(pl.multiple_of(STEP * (1 - core), 8), HALF)
    mine = pl.ds(pl.multiple_of(STEP * core, 8), HALF)
    lpack[...] = packed(1 - core)
    swap = [send(0, acc.at[theirs, pl.ds(0, 256)], ra, sibling), send(1, lpack, ral, sibling)]
    for c in swap:
        c.start()
    own_left = packed(core)
    for c in swap:
        c.wait_recv()
    q0 = acc[mine, :128] + ra[:, :128]
    q1 = acc[mine, 128:256] + ra[:, 128:]
    ql = own_left + ral[...]
    q_ref[0], q_ref[1], ql_ref[...] = q0, q1, ql

    cross = [send(2, q_ref.at[1 - chip], rq, beside), send(3, ql_ref, rql, beside)]
    for c in cross:
        c.start()
    hi, lo = split(jnp.concatenate([q0, q1, unpacked(ql)], axis=1))
    edges = jnp.dot(hi, hot_send[...], preferred_element_type=F32) + jnp.dot(
        lo, hot_send[...], preferred_element_type=F32
    )
    ht[0], ht[1] = edges[:, :128], edges[:, 128:]
    heads = [send(4 + i, ht.at[0], hr.at[chip], peers[4 + i], 4 + chip) for i in range(2)]
    tails = send(6, ht.at[1], tr.at[chip], (up, core), 6 + chip)
    for c in (heads[1], tails, heads[0]):
        c.start()
    for c in cross:
        c.wait_recv()
    s = slot_of_column(iota((1, 128), 1) + 128 * chip)
    box1 = os1 + s
    keep = (box1 >= gs1) & (box1 < gs2) & (box1 < os2)
    own = jnp.where(keep, q_ref[chip] + rq[...], 0.0)
    box1 = os1 + slot_of_column(256 + (iota((1, 128), 1) & 31))
    keep = (box1 >= gs1) & (box1 < gs2) & (box1 < os2)
    own_left = unpacked(jnp.where(keep, ql_ref[...] + rql[...], 0.0))
    for i in range(2):
        send(4 + i, ht.at[0], hr.at[i], peers[4], 4 + i).wait_recv()

    @pl.when(chip == 0)
    def _():
        for i in range(2):
            send(6, ht.at[1], tr.at[i], peers[4], 6 + i).wait_recv()

    @pl.when(chip == 1)
    def _():
        tr[...] = jnp.zeros(tr.shape, F32)

    hi, lo = split(jnp.concatenate([hr[0] + hr[1], tr[0] + tr[1]], axis=1))
    moved = jnp.dot(hi, hot_recv[...], preferred_element_type=F32) + jnp.dot(
        lo, hot_recv[...], preferred_element_type=F32
    )
    v0, v1 = own + moved[:, :128], own_left + moved[:, 128:]
    v_ref[0], v_ref[1] = v0, v1
    last = send(8, v_ref, fr, sibling)
    last.start()
    for i, v in enumerate((v0, v1)):
        fin[i, mine] = v
    last.wait_recv()
    for i in range(2):
        fin[i, theirs] = fr[i]
        tt[i] = fin[i].T
    out[0:64] = tt[0, pl.ds(pl.multiple_of(64 * core, 8), 64), :F]
    out[64:72] = tt[1, pl.ds(pl.multiple_of(8 * o, 8), 8), :F]

    for c in (to_beside, to_sibling, *(to_prev_segment(i) for i in range(2))):
        c.wait_send()
    for i, there in enumerate(passed):
        hand_on(1 + i, there).wait_send()

    @pl.when(core == 0)
    def _():
        hand_on(5, 10, SHORT).wait_send()

    @pl.when(o < 2)
    def _():
        for i in range(2):
            to_next_segment(i, TILES).wait_send()

    @pl.when(o == 2)
    def _():
        for i in range(2):
            to_next_segment(i, SHORT).wait_send()

    for c in (*swap, *cross, *heads, tails, last):
        c.wait_send()


def body(density, operators, owner_count, group_count, target_slot, source_box):
    vmem = pl.BlockSpec(memory_space=pltpu.VMEM)
    scratch = [
        pltpu.VMEM((12, TILES, 8, 128), F32),
        pltpu.VMEM((2, 304, F), F32),
        pltpu.VMEM((OFFS // 2, 304, KP), BF16),
        pltpu.VMEM((WIN, 384), F32),
        pltpu.VMEM((592, WIN), BF16),
        pltpu.VMEM((OFFS, 256), I32),
        pltpu.VMEM((2, 256), I32),
        pltpu.VMEM((OFFS // 2, KP, 384), BF16),
        pltpu.VMEM((304, 384), F32),
        pltpu.VMEM((304, 128), F32),
        pltpu.VMEM((384, 256), BF16),
        pltpu.VMEM((256, 256), BF16),
        pltpu.VMEM((40, 128), F32),
        pltpu.VMEM((HALF, 256), F32),
        pltpu.VMEM((40, 128), F32),
        pltpu.VMEM((2, HALF, 128), F32),
        pltpu.VMEM((40, 128), F32),
        pltpu.VMEM((2, HALF, 128), F32),
        pltpu.VMEM((HALF, 128), F32),
        pltpu.VMEM((40, 128), F32),
        pltpu.VMEM((2, HALF, 128), F32),
        pltpu.VMEM((2, HALF, 128), F32),
        pltpu.VMEM((2, HALF, 128), F32),
        pltpu.VMEM((2, HALF, 128), F32),
        pltpu.VMEM((2, 384, 128), F32),
        pltpu.VMEM((2, 128, 384), F32),
        pltpu.SemaphoreType.DMA((2,)),
        pltpu.SemaphoreType.DMA((5,)),
        pltpu.SemaphoreType.DMA((6,)),
        pltpu.SemaphoreType.DMA((12,)),
        pltpu.SemaphoreType.DMA((9,)),
        pltpu.SemaphoreType.DMA((9,)),
    ]
    return pl.pallas_call(
        kernel,
        out_shape=jax.ShapeDtypeStruct((ROWS, F), F32),
        in_specs=[vmem, pl.BlockSpec(memory_space=pl.ANY), vmem, vmem, vmem, vmem],
        out_specs=vmem,
        scratch_shapes=scratch,
        compiler_params=pltpu.CompilerParams(
            collective_id=0, has_side_effects=True, vmem_limit_bytes=48 * 2**20
        ),
        name="translate",
    )(density, operators, owner_count[None], group_count[None], target_slot, source_box)


def solution(mesh):
    placed = (P(("box", "op"), None), P("op", None, None), P(), P(), P("box", "op", None), P("box", "op", None))
    return jax.shard_map(
        body, mesh=mesh, in_specs=placed, out_specs=P(("box", "op"), None), check_vma=False
    )
```

time: 121 us -> 55 us (0.45)
  the two profiles are of different devices: /device:TPU:253 before, /device:TPU:1 now
where the time goes in v1:
time: 55 us; the launch traced here: 54.5 us
  Pallas kernels  50.2 us (91%)
  local copies, waits for them, and re-layouts  4.33 us (8%)
    pallas_call x1, Pallas kernels, body(): pl.pallas_call(kernel, out_shape=jax.ShapeDtypeStruct((ROWS, F), F32), in...  50.2 us
    unnamed x11, local copies, waits for them, and re-layouts  4.33 us

profile of v1, /device:TPU:1, one launch (start us, length us, event | category | flops | bytes accessed | tf_op | source)
XLA Modules:
  0.0 54.5 jit_solution(5092366644765814579)
XLA Ops:
  0.0 0.0 copy-start
  0.0 0.9 %copy-done = f32[72,296]{1,0:T(8,128)S(1)} copy-done((f32[72,296]{1,0:T(8,128)S(1)}, f32[72,296]{1,0:T(8,128)}, u32[]{:S(2)}) %copy-start) | copy-done | bytes 85272
  0.9 0.0 copy-start.1
  0.9 0.7 %copy-done.1 = s32[1,16,288]{2,1,0:T(8,128)S(1)} copy-done((s32[1,16,288]{2,1,0:T(8,128)S(1)}, s32[1,16,288]{2,1,0:T(8,128)}, u32[]{:S(2)}) %copy-start.1) | copy-done | bytes 18456
  1.6 0.0 copy-start.2
  1.6 0.7 %copy-done.2 = s32[1,16,288]{2,1,0:T(8,128)S(1)} copy-done((s32[1,16,288]{2,1,0:T(8,128)S(1)}, s32[1,16,288]{2,1,0:T(8,128)}, u32[]{:S(2)}) %copy-start.2) | copy-done | bytes 18456
  2.4 0.0 copy-start.3
  2.4 0.7 %copy-done.3 = s32[128]{0:T(128)S(1)} copy-done((s32[128]{0:T(128)S(1)}, s32[128]{0:T(128)}, u32[]{:S(2)}) %copy-start.3) | copy-done | bytes 536
  3.0 0.0 copy-start.4
  3.0 0.7 %copy-done.4 = s32[128]{0:T(128)S(1)} copy-done((s32[128]{0:T(128)S(1)}, s32[128]{0:T(128)}, u32[]{:S(2)}) %copy-start.4) | copy-done | bytes 536
  3.7 50.2 %translate.1 = f32[72,296]{1,0:T(8,128)S(1)} custom-call(f32[72,296]{1,0:T(8,128)S(1)} %copy-done, f32[16,296,296]{2,1,0:T(8,128)} %ops.1, s32[1,128]{1,0:T(1,128)S(1)} %bitcast.2, s32[1,128]{1,0:T(1,128)S(1)} %bitcast.3, s32[1,16,288]{2,1,0:T(8,128)S(1)} %copy-done.1, s32[1,16,288]{2,1,0:T(8,128)S(1)} %copy-done.2), custom_call_target="tpu_custom_call" | custom-call | tf_op jit(solution)/shard_map/translate/pallas_call | solution.py:404
  53.8 0.6 %copy.8 = f32[72,296]{1,0:T(8,128)} copy(f32[72,296]{1,0:T(8,128)S(1)} %translate.1) | data formatting | bytes 170496
Async XLA Ops:
  0.0 0.9 %copy-start = (f32[72,296]{1,0:T(8,128)S(1)}, f32[72,296]{1,0:T(8,128)}, u32[]{:S(2)}) copy-start(f32[72,296]{1,0:T(8,128)} %den.1) | copy-start | bytes 255748
  0.9 0.7 %copy-start.1 = (s32[1,16,288]{2,1,0:T(8,128)S(1)}, s32[1,16,288]{2,1,0:T(8,128)}, u32[]{:S(2)}) copy-start(s32[1,16,288]{2,1,0:T(8,128)} %tgt.1) | copy-start | bytes 55300
  1.6 0.7 %copy-start.2 = (s32[1,16,288]{2,1,0:T(8,128)S(1)}, s32[1,16,288]{2,1,0:T(8,128)}, u32[]{:S(2)}) copy-start(s32[1,16,288]{2,1,0:T(8,128)} %src.1) | copy-start | bytes 55300
  2.4 0.7 %copy-start.3 = (s32[128]{0:T(128)S(1)}, s32[128]{0:T(128)}, u32[]{:S(2)}) copy-start(s32[128]{0:T(128)} %param.8) | copy-start | bytes 1540
  3.0 0.7 %copy-start.4 = (s32[128]{0:T(128)S(1)}, s32[128]{0:T(128)}, u32[]{:S(2)}) copy-start(s32[128]{0:T(128)} %param.9) | copy-start | bytes 1540

commit v2 on v1

--- a/solution.py
+++ b/solution.py
@@ -17,7 +17,6 @@
 TILES = 21
 SHORT = 15
 WIN = 768
-KP = 1792
 
 
 def iota(shape, dim):
@@ -43,10 +42,10 @@
 
 
 def kernel(
-    den, ops, ocnt, gcnt, tgt, src, out,
-    rx, stage, o_all, x_rows, xt, pmain, pleft, g_all, acc, ufold,
+    den_hbm, ops, ocnt_hbm, gcnt_hbm, tgt_hbm, src_hbm, out,
+    den, ocnt, gcnt, tgt, src, rx, stage, o_main, o_left, xt, pmain, pleft, g_hi, g_lo, g_last, acc, ufold,
     hot_send, hot_recv, lpack, ra, ral, q_ref, ql_ref, ht, rq, rql, hr, tr, v_ref, fr, fin, tt,
-    op_sem, ici_send, sib_send, rsem, osend, orecv,
+    in_sem, op_sem, ici_send, sib_send, rsem, osend, orecv,
 ):
     b, o = lax.axis_index("box"), lax.axis_index("op")
     n = lax.axis_size("box")
@@ -56,13 +55,19 @@
     sibling, beside = (b, sib), (b, far)
     peers = [sibling, beside, (up, o), (up, far), (down, o), (down, far)]
 
-    def op_copy(k, slot):
-        return pltpu.make_async_copy(ops.at[k], stage.at[slot, pl.ds(0, F)], op_sem.at[slot])
-
-    op_copy(0, 0).start()
+    def op_copy(k):
+        return pltpu.make_async_copy(ops.at[k], stage.at[k, pl.ds(0, F)], op_sem.at[k])
+
     barrier = pltpu.get_barrier_semaphore()
     for peer in peers:
         pl.semaphore_signal(barrier, inc=1, device_id=peer, device_id_type=MESH)
+    pairs = ((den_hbm, den), (ocnt_hbm, ocnt), (gcnt_hbm, gcnt), (tgt_hbm, tgt), (src_hbm, src))
+    inputs = [pltpu.make_async_copy(a, v, in_sem.at[i]) for i, (a, v) in enumerate(pairs)]
+    for c in inputs:
+        c.start()
+    for k in range(OFFS):
+        op_copy(k).start()
+    inputs[0].wait()
 
     me = 4 + o
     for lt in range(3):
@@ -102,12 +107,14 @@
     to_beside.start()
     to_sibling.start()
 
+    for c in inputs[1:]:
+        c.wait()
     counts_o, counts_g = ocnt[...], gcnt[...]
     os0, os1, os2 = (start_at(counts_o, b + i) for i in (-1, 0, 1))
     gs1, gs2 = (start_at(counts_g, b + i) for i in (0, 1))
     shift = gs1 - os1
     m = src[0]
-    place = jnp.where(m < os1, m - os0, jnp.where(m < os2, CAP + m - os1, 2 * CAP + m - os2))
+    place = jnp.where(m < os1, m - os0 + 480, jnp.where(m < os2, m - os1, m - os2 + CAP))
     place = jnp.where(tgt[0] < CAP, place, -1)
     j = iota((CAP, 384), 0) + shift
     j = jnp.where(j < 0, j + CAP, jnp.where(j >= CAP, j - CAP, j))
@@ -141,30 +148,21 @@
     hot_recv[:, :128] = jnp.where(known & (slot == slot_of_column(lane + 128 * chip)), 1.0, 0.0).astype(BF16)
     hot_recv[:, 128:] = jnp.where(known & (lane < 32) & (slot == slot_of_column(lane + 256)), 1.0, 0.0).astype(BF16)
 
-    stage[:, pl.ds(F, 8), :] = jnp.zeros((2, 8, F), F32)
+    stage[:, pl.ds(F, 8), :] = jnp.zeros((OFFS, 8, F), F32)
 
     def split_pair(q, _):
         for par in range(2):
             k = 2 * q + par
-
-            @pl.when(k < OFFS - 1)
-            def _():
-                op_copy(k + 1, 1 - par).start()
-
-            op_copy(k, par).wait()
-            v = stage[par]
+            op_copy(k).wait()
+            v = stage[k]
             hi = v.astype(BF16)
             hi32 = hi.astype(F32)
             lo32 = v - hi32
-            base = 768 * par
-            o_all[q, :, base : base + 256] = hi[:, :256]
-            o_all[q, :, base + 256 : base + 512] = hi[:, :256]
-            o_all[q, :, base + 512 : base + 768] = lo32[:, :256].astype(BF16)
+            o_main[q, :304, 256 * par : 256 * par + 256] = hi[:, :256]
+            o_main[q, 304:, 256 * par : 256 * par + 256] = lo32[:, :256].astype(BF16)
             last = jnp.concatenate([hi32[:, 256:], hi32[:, 256:], lo32[:, 256:], jnp.zeros((304, 8), F32)], axis=1)
-            o_all[q, :, 1536 + 128 * par : 1664 + 128 * par] = last.astype(BF16)
+            o_left[q, :, 128 * par : 128 * par + 128] = last.astype(BF16)
         return 0
-
-    lax.fori_loop(0, OFFS // 2, split_pair, 0)
 
     def arrived(there, count=TILES):
         block_copy(there, there, count, ici_send.at[0], sibling).wait_recv()
@@ -172,87 +170,106 @@
     def hand_on(i, there, count=TILES):
         return block_copy(there, there, count, sib_send.at[i], sibling)
 
-    passed = [4 + far, o, far, 8 + core]
-    for i, there in enumerate(passed):
-        arrived(there)
-        hand_on(1 + i, there).start()
-
-    @pl.when(core == 0)
-    def _():
-        arrived(10, SHORT)
-        hand_on(5, 10, SHORT).start()
-
-    for there in (4 + sib, 4 + (sib + 2) % 4, sib, (sib + 2) % 4, 8 + 1 - core):
-        arrived(there)
-
-    @pl.when(core == 1)
-    def _():
-        arrived(10, SHORT)
-
-    def unpack(idx, rts):
-        base = pl.multiple_of(ROWS * idx, 8)
-        for rt in rts:
-            at = pl.ds(base + 8 * rt, 8)
-            for h in range(2):
-                x_rows[at, 128 * h : 128 * h + 128] = rx[idx, 3 + 2 * rt + h]
-            g = rt // 3
-            left = rx[idx, rt % 3]
-            x_rows[at, 256:384] = pltpu.roll(left, 128 - 40 * g, 1) if g else left
-
-    def unpack_full(idx, _):
-        unpack(idx, range(9))
-        return 0
-
-    lax.fori_loop(0, 10, unpack_full, 0)
-    unpack(10, range(6))
-
-    for i in range(WIN // 128):
-        t = x_rows[128 * i : 128 * i + 128, :].T
+    def pass_own():
+        arrived(4 + far)
+        hand_on(1, 4 + far).start()
+
+    def pass_prev():
+        for i, there in ((2, o), (3, far)):
+            arrived(there)
+            hand_on(i, there).start()
+
+    def pass_next():
+        arrived(8 + core)
+        hand_on(4, 8 + core).start()
+
+        @pl.when(core == 0)
+        def _():
+            arrived(10, SHORT)
+            hand_on(5, 10, SHORT).start()
+
+    order = [(idx, rt) for idx in (4, 5, 6, 7, 8, 9, 10, 0, 1, 2, 3) for rt in range(6 if idx == 10 else 9)]
+
+    def turn_rows(i):
+        tiles = order[16 * i : 16 * i + 16]
+        wide = [jnp.concatenate([rx[idx, 3 + 2 * rt + h] for idx, rt in tiles], axis=0).T for h in range(2)]
+        left = [
+            pltpu.roll(rx[idx, rt % 3], 128 - 40 * (rt // 3), 1) if rt >= 3 else rx[idx, rt % 3] for idx, rt in tiles
+        ]
+        t = jnp.concatenate([*wide, jnp.concatenate(left, axis=0).T[:40]], axis=0)
         hi32 = t.astype(BF16).astype(F32)
         lo32 = t - hi32
         xt[:, 128 * i : 128 * i + 128] = jnp.concatenate(
             [hi32[:256], lo32[:256], hi32[256:F], lo32[256:F]], axis=0
         ).astype(BF16)
 
-    def gathered(row):
-        hot = jnp.where(iota((WIN, 256), 0) == row, 1.0, 0.0).astype(BF16)
-        return jnp.dot(xt[...], hot, preferred_element_type=F32)
-
-    def last_rows(g):
-        return jnp.concatenate([g[512:592], g[512:552], jnp.zeros((8, g.shape[1]), F32)], axis=0).astype(BF16)
-
-    def gather_pair(q, _):
-        for par in range(2):
-            g = gathered(pmain[pl.ds(2 * q + par, 1), :])
-            hi, lo = g[:256].astype(BF16), g[256:512].astype(BF16)
-            base = 768 * par
-            g_all[q, base : base + 256, :256] = hi
-            g_all[q, base + 256 : base + 512, :256] = lo
-            g_all[q, base + 512 : base + 768, :256] = hi
-            g_all[q, 1536 + 128 * par : 1664 + 128 * par, :256] = last_rows(g)
-        return 0
-
-    lax.fori_loop(0, OFFS // 2, gather_pair, 0)
-
-    def gather_left(t, _):
-        g = gathered(pleft[pl.ds(t, 1), :])
-        for kk in range(8):
-            h, a = kk // 4, kk % 4
-            part = jnp.where(group_of_lane == a, g[:, 128 * h : 128 * h + 128], 0.0)
-            hi, lo = part[:256].astype(BF16), part[256:512].astype(BF16)
-            q, base = 4 * t + kk // 2, 768 * (kk % 2)
-            g_all[q, base : base + 256, 256:] = hi
-            g_all[q, base + 256 : base + 512, 256:] = lo
-            g_all[q, base + 512 : base + 768, 256:] = hi
-            g_all[q, 1536 + 128 * (kk % 2) : 1664 + 128 * (kk % 2), 256:] = last_rows(part)
-        return 0
-
-    lax.fori_loop(0, 2, gather_left, 0)
-
-    acc[...] = jnp.dot(o_all[0], g_all[0], preferred_element_type=F32)
+    def gathered(row, first, last):
+        hot = jnp.where(iota((last - first, 256), 0) + first == row, 1.0, 0.0).astype(BF16)
+        return jnp.dot(xt[:, first:last], hot, preferred_element_type=F32)
+
+    def put(q, par, columns, g, add):
+        tail = jnp.concatenate([g[512:592], g[512:552], jnp.zeros((8, g.shape[1]), F32)], axis=0)
+        for ref, at, v in (
+            (g_hi, pl.ds(256 * par, 256), g[:256]),
+            (g_lo, pl.ds(256 * par, 256), g[256:512]),
+            (g_last, pl.ds(128 * par, 128), tail),
+        ):
+            v = v.astype(BF16)
+            ref[q, at, columns] = ref[q, at, columns] + v if add else v
+
+    def gather(first, last):
+        add = first > 0
+
+        def gather_pair(q, _):
+            for par in range(2):
+                put(q, par, pl.ds(0, 256), gathered(pmain[pl.ds(2 * q + par, 1), :], first, last), add)
+            return 0
+
+        lax.fori_loop(0, OFFS // 2, gather_pair, 0)
+
+        def gather_left(t, _):
+            g = gathered(pleft[pl.ds(t, 1), :], first, last)
+            for kk in range(8):
+                h, a = kk // 4, kk % 4
+                part = jnp.where(group_of_lane == a, g[:, 128 * h : 128 * h + 128], 0.0)
+                put(4 * t + kk // 2, kk % 2, pl.ds(256, 128), part, add)
+            return 0
+
+        lax.fori_loop(0, 2, gather_left, 0)
+
+    lax.fori_loop(0, OFFS // 4, split_pair, 0)
+    pass_own()
+    lax.fori_loop(OFFS // 4, OFFS // 2, split_pair, 0)
+    even = b % 2 == 0
+    pl.when(even)(pass_next)
+    pl.when(jnp.logical_not(even))(pass_prev)
+    arrived(4 + sib)
+    arrived(4 + (sib + 2) % 4)
+    turn_rows(0)
+    turn_rows(1)
+    gather(0, 256)
+    pl.when(even)(pass_prev)
+    pl.when(jnp.logical_not(even))(pass_next)
+    for there in (sib, (sib + 2) % 4, 9 - core):
+        arrived(there)
+
+    @pl.when(core == 1)
+    def _():
+        arrived(10, SHORT)
+
+    for i in range(2, WIN // 128):
+        turn_rows(i)
+    gather(256, WIN)
+
+    def product(q):
+        both = jnp.dot(o_main[q], g_hi[q], preferred_element_type=F32)
+        third = jnp.dot(o_main[q, :304], g_lo[q], preferred_element_type=F32)
+        return both[:304] + both[304:] + third + jnp.dot(o_left[q], g_last[q], preferred_element_type=F32)
+
+    acc[...] = product(0)
 
     def multiply(q, _):
-        acc[...] += jnp.dot(o_all[q], g_all[q], preferred_element_type=F32)
+        acc[...] += product(q)
         return 0
 
     lax.fori_loop(1, OFFS // 2, multiply, 0)
@@ -344,7 +361,7 @@
 
     for c in (to_beside, to_sibling, *(to_prev_segment(i) for i in range(2))):
         c.wait_send()
-    for i, there in enumerate(passed):
+    for i, there in enumerate((4 + far, o, far, 8 + core)):
         hand_on(1 + i, there).wait_send()
 
     @pl.when(core == 0)
@@ -368,14 +385,21 @@
 def body(density, operators, owner_count, group_count, target_slot, source_box):
     vmem = pl.BlockSpec(memory_space=pltpu.VMEM)
     scratch = [
+        pltpu.VMEM((ROWS, F), F32),
+        pltpu.VMEM(owner_count[None].shape, I32),
+        pltpu.VMEM(group_count[None].shape, I32),
+        pltpu.VMEM((1, OFFS, CAP), I32),
+        pltpu.VMEM((1, OFFS, CAP), I32),
         pltpu.VMEM((12, TILES, 8, 128), F32),
-        pltpu.VMEM((2, 304, F), F32),
-        pltpu.VMEM((OFFS // 2, 304, KP), BF16),
-        pltpu.VMEM((WIN, 384), F32),
+        pltpu.VMEM((OFFS, 304, F), F32),
+        pltpu.VMEM((OFFS // 2, 608, 512), BF16),
+        pltpu.VMEM((OFFS // 2, 304, 256), BF16),
         pltpu.VMEM((592, WIN), BF16),
         pltpu.VMEM((OFFS, 256), I32),
         pltpu.VMEM((2, 256), I32),
-        pltpu.VMEM((OFFS // 2, KP, 384), BF16),
+        pltpu.VMEM((OFFS // 2, 512, 384), BF16),
+        pltpu.VMEM((OFFS // 2, 512, 384), BF16),
+        pltpu.VMEM((OFFS // 2, 256, 384), BF16),
         pltpu.VMEM((304, 384), F32),
         pltpu.VMEM((304, 128), F32),
         pltpu.VMEM((384, 256), BF16),
@@ -394,7 +418,8 @@
         pltpu.VMEM((2, HALF, 128), F32),
         pltpu.VMEM((2, 384, 128), F32),
         pltpu.VMEM((2, 128, 384), F32),
-        pltpu.SemaphoreType.DMA((2,)),
+        pltpu.SemaphoreType.DMA((5,)),
+        pltpu.SemaphoreType.DMA((OFFS,)),
         pltpu.SemaphoreType.DMA((5,)),
         pltpu.SemaphoreType.DMA((6,)),
         pltpu.SemaphoreType.DMA((12,)),
@@ -404,11 +429,11 @@
     return pl.pallas_call(
         kernel,
         out_shape=jax.ShapeDtypeStruct((ROWS, F), F32),
-        in_specs=[vmem, pl.BlockSpec(memory_space=pl.ANY), vmem, vmem, vmem, vmem],
+        in_specs=[pl.BlockSpec(memory_space=pltpu.HBM)] * 6,
         out_specs=vmem,
         scratch_shapes=scratch,
         compiler_params=pltpu.CompilerParams(
-            collective_id=0, has_side_effects=True, vmem_limit_bytes=48 * 2**20
+            collective_id=0, has_side_effects=True, vmem_limit_bytes=60 * 2**20
         ),
         name="translate",
     )(density, operators, owner_count[None], group_count[None], target_slot, source_box)

time: 55 us -> 53 us (0.964)
  local copies, waits for them, and re-layouts: 4.33 us -> 1.55 us
  Pallas kernels: 50.2 us -> 51.3 us
    unnamed x11 -> x1, local copies, waits for them, and re-layouts: 4.33 us -> 1.55 us
    pallas_call x1, Pallas kernels: 50.2 us -> 51.3 us  [body(): pl.pallas_call(kernel, out_shape=jax.ShapeDtypeStruct((ROWS, F), F32), in...]
where the time goes in v2:
time: 53 us; the launch traced here: 52.8 us
  Pallas kernels  51.3 us (97%)
  local copies, waits for them, and re-layouts  1.55 us (3%)
    pallas_call x1, Pallas kernels, body(): pl.pallas_call(kernel, out_shape=jax.ShapeDtypeStruct((ROWS, F), F32), in...  51.3 us
    unnamed x1, local copies, waits for them, and re-layouts  1.55 us

profile of v2, /device:TPU:1, one launch (start us, length us, event | category | flops | bytes accessed | tf_op | source)
XLA Modules:
  0.0 52.8 jit_solution(6034296840915044638)
XLA Ops:
  0.0 51.3 %translate.1 = f32[72,296]{1,0:T(8,128)} custom-call(f32[72,296]{1,0:T(8,128)} %den_hbm.1, f32[16,296,296]{2,1,0:T(8,128)} %ops.1, s32[1,128]{1,0:T(1,128)} %bitcast.2, s32[1,128]{1,0:T(1,128)} %bitcast.3, s32[1,16,288]{2,1,0:T(8,128)} %tgt_hbm.1, s32[1,16,288]{2,1,0:T(8,128)} %src_hbm.1), custom_call_target="tpu_custom_call" | custom-call | tf_op jit(solution)/shard_map/translate/pallas_call | solution.py:429
  51.3 1.5 %copy.8 = f32[72,296]{1,0:T(8,128)} copy(f32[72,296]{1,0:T(8,128)} %translate.1) | data formatting | bytes 170496

commit v3 on v2

--- a/solution.py
+++ b/solution.py
@@ -16,7 +16,6 @@
 OFFS = 16
 TILES = 21
 SHORT = 15
-WIN = 768
 
 
 def iota(shape, dim):
@@ -77,36 +76,6 @@
         for h in range(2):
             rx[me, 3 + 2 * rt + h] = den[8 * rt : 8 * rt + 8, 128 * h : 128 * h + 128]
 
-    def block_copy(here, there, count, send, device):
-        return pltpu.make_async_remote_copy(
-            src_ref=rx.at[here, pl.ds(0, count)], dst_ref=rx.at[there, pl.ds(0, count)],
-            send_sem=send, recv_sem=rsem.at[there], device_id=device, device_id_type=MESH,
-        )
-
-    pl.semaphore_wait(barrier, len(peers))
-
-    def to_prev_segment(i):
-        return block_copy(me, o, TILES, ici_send.at[1 + i], peers[2 + i])
-
-    def to_next_segment(i, count):
-        return block_copy(me, 8 + o, count, ici_send.at[3 + i], peers[4 + i])
-
-    to_beside = block_copy(me, me, TILES, ici_send.at[0], beside)
-    to_sibling = block_copy(me, me, TILES, sib_send.at[0], sibling)
-    for i in (1, 0):
-        to_prev_segment(i).start()
-
-        @pl.when(o < 2)
-        def _():
-            to_next_segment(i, TILES).start()
-
-        @pl.when(o == 2)
-        def _():
-            to_next_segment(i, SHORT).start()
-
-    to_beside.start()
-    to_sibling.start()
-
     for c in inputs[1:]:
         c.wait()
     counts_o, counts_g = ocnt[...], gcnt[...]
@@ -114,7 +83,10 @@
     gs1, gs2 = (start_at(counts_g, b + i) for i in (0, 1))
     shift = gs1 - os1
     m = src[0]
-    place = jnp.where(m < os1, m - os0 + 480, jnp.where(m < os2, m - os1, m - os2 + CAP))
+    before, own = m - os0, m - os1
+    before = 512 + jnp.where(before < 256, before, before - 256)
+    own = jnp.where(own < 256, own, own + 192)
+    place = jnp.where(m < os1, before, jnp.where(m < os2, own, 256 + m - os2))
     place = jnp.where(tgt[0] < CAP, place, -1)
     j = iota((CAP, 384), 0) + shift
     j = jnp.where(j < 0, j + CAP, jnp.where(j >= CAP, j - CAP, j))
@@ -122,7 +94,8 @@
     turned = jnp.dot(place.astype(F32), turn, precision=lax.Precision.HIGHEST, preferred_element_type=F32)
     turned = (turned + 0.25 * jnp.where(turned < 0, -1.0, 1.0)).astype(I32)
     pmain[...] = turned[:, :256]
-    group_of_lane = iota((1, 128), 1) >> 5
+    lane_id = iota((1, 128), 1)
+    group_of_lane = lane_id >> 5
     for t in range(2):
         rows = []
         for h in range(2):
@@ -148,6 +121,36 @@
     hot_recv[:, :128] = jnp.where(known & (slot == slot_of_column(lane + 128 * chip)), 1.0, 0.0).astype(BF16)
     hot_recv[:, 128:] = jnp.where(known & (lane < 32) & (slot == slot_of_column(lane + 256)), 1.0, 0.0).astype(BF16)
 
+    def block_copy(here, there, count, send, device):
+        return pltpu.make_async_remote_copy(
+            src_ref=rx.at[here, pl.ds(0, count)], dst_ref=rx.at[there, pl.ds(0, count)],
+            send_sem=send, recv_sem=rsem.at[there], device_id=device, device_id_type=MESH,
+        )
+
+    pl.semaphore_wait(barrier, len(peers))
+
+    def to_prev_segment(i):
+        return block_copy(me, o, TILES, ici_send.at[1 + i], peers[2 + i])
+
+    def to_next_segment(i, count):
+        return block_copy(me, 8 + o, count, ici_send.at[3 + i], peers[4 + i])
+
+    to_beside = block_copy(me, me, TILES, ici_send.at[0], beside)
+    to_sibling = block_copy(me, me, TILES, sib_send.at[0], sibling)
+    for i in (1, 0):
+        to_prev_segment(i).start()
+
+        @pl.when(o < 2)
+        def _():
+            to_next_segment(i, TILES).start()
+
+        @pl.when(o == 2)
+        def _():
+            to_next_segment(i, SHORT).start()
+
+    to_beside.start()
+    to_sibling.start()
+
     stage[:, pl.ds(F, 8), :] = jnp.zeros((OFFS, 8, F), F32)
 
     def split_pair(q, _):
@@ -188,24 +191,43 @@
             arrived(10, SHORT)
             hand_on(5, 10, SHORT).start()
 
-    order = [(idx, rt) for idx in (4, 5, 6, 7, 8, 9, 10, 0, 1, 2, 3) for rt in range(6 if idx == 10 else 9)]
-
-    def turn_rows(i):
-        tiles = order[16 * i : 16 * i + 16]
-        wide = [jnp.concatenate([rx[idx, 3 + 2 * rt + h] for idx, rt in tiles], axis=0).T for h in range(2)]
-        left = [
-            pltpu.roll(rx[idx, rt % 3], 128 - 40 * (rt // 3), 1) if rt >= 3 else rx[idx, rt % 3] for idx, rt in tiles
-        ]
-        t = jnp.concatenate([*wide, jnp.concatenate(left, axis=0).T[:40]], axis=0)
-        hi32 = t.astype(BF16).astype(F32)
-        lo32 = t - hi32
-        xt[:, 128 * i : 128 * i + 128] = jnp.concatenate(
+    def row_tiles(segment, tiles):
+        return [(4 * segment + r // 9, r % 9) for r in tiles]
+
+    def wide_left(idx, rt):
+        left = rx[idx, rt % 3]
+        return rx[idx, 3 + 2 * rt], rx[idx, 4 + 2 * rt], pltpu.roll(left, 128 - 40 * (rt // 3), 1) if rt >= 3 else left
+
+    def turn_rows(t, half, parts):
+        cols = [jnp.concatenate(list(p), axis=0).T for p in zip(*parts)]
+        v = jnp.concatenate([cols[0], cols[1], cols[2][:40]], axis=0)
+        hi32 = v.astype(BF16).astype(F32)
+        lo32 = v - hi32
+        xt[t, :, 128 * half : 128 * half + 128] = jnp.concatenate(
             [hi32[:256], lo32[:256], hi32[256:F], lo32[256:F]], axis=0
         ).astype(BF16)
 
-    def gathered(row, first, last):
-        hot = jnp.where(iota((last - first, 256), 0) + first == row, 1.0, 0.0).astype(BF16)
-        return jnp.dot(xt[:, first:last], hot, preferred_element_type=F32)
+    def turn_own():
+        for half in range(2):
+            turn_rows(0, half, [wide_left(*a) for a in row_tiles(1, range(16 * half, 16 * half + 16))])
+
+    def turn_next():
+        turn_rows(1, 0, [wide_left(*a) for a in row_tiles(2, range(16))])
+        parts = [wide_left(*a) for a in row_tiles(2, range(16, 24)) + row_tiles(1, range(32, 36))]
+        turn_rows(1, 1, parts + [(jnp.zeros((8, 128), F32),) * 3] * 4)
+
+    def turn_prev():
+        parts = [wide_left(*a) for a in row_tiles(0, range(16))]
+        folded = [wide_left(*a) for a in row_tiles(0, range(32, 36))]
+        long = os1 - os0 > 256
+        for r in range(4):
+            parts[r] = tuple(jnp.where(long, x, y) for x, y in zip(folded[r], parts[r]))
+        turn_rows(2, 0, parts)
+        turn_rows(2, 1, [wide_left(*a) for a in row_tiles(0, range(16, 32))])
+
+    def gathered(row, t):
+        hot = jnp.where(iota((256, 256), 0) + 256 * t == row, 1.0, 0.0).astype(BF16)
+        return jnp.dot(xt[t], hot, preferred_element_type=F32)
 
     def put(q, par, columns, g, add):
         tail = jnp.concatenate([g[512:592], g[512:552], jnp.zeros((8, g.shape[1]), F32)], axis=0)
@@ -217,22 +239,20 @@
             v = v.astype(BF16)
             ref[q, at, columns] = ref[q, at, columns] + v if add else v
 
-    def gather(first, last):
-        add = first > 0
-
+    def gather(t, add):
         def gather_pair(q, _):
             for par in range(2):
-                put(q, par, pl.ds(0, 256), gathered(pmain[pl.ds(2 * q + par, 1), :], first, last), add)
+                put(q, par, pl.ds(0, 256), gathered(pmain[pl.ds(2 * q + par, 1), :], t), add)
             return 0
 
         lax.fori_loop(0, OFFS // 2, gather_pair, 0)
 
-        def gather_left(t, _):
-            g = gathered(pleft[pl.ds(t, 1), :], first, last)
+        def gather_left(i, _):
+            g = gathered(pleft[pl.ds(i, 1), :], t)
             for kk in range(8):
                 h, a = kk // 4, kk % 4
                 part = jnp.where(group_of_lane == a, g[:, 128 * h : 128 * h + 128], 0.0)
-                put(4 * t + kk // 2, kk % 2, pl.ds(256, 128), part, add)
+                put(4 * i + kk // 2, kk % 2, pl.ds(256, 128), part, add)
             return 0
 
         lax.fori_loop(0, 2, gather_left, 0)
@@ -242,41 +262,51 @@
     lax.fori_loop(OFFS // 4, OFFS // 2, split_pair, 0)
     even = b % 2 == 0
     pl.when(even)(pass_next)
-    pl.when(jnp.logical_not(even))(pass_prev)
+    odd = jnp.logical_not(even)
+    pl.when(odd)(pass_prev)
+
+    def took_prev():
+        arrived(sib)
+        arrived((sib + 2) % 4)
+        turn_prev()
+
+    def took_next():
+        arrived(9 - core)
+
+        @pl.when(core == 1)
+        def _():
+            arrived(10, SHORT)
+
+        turn_next()
+
     arrived(4 + sib)
     arrived(4 + (sib + 2) % 4)
-    turn_rows(0)
-    turn_rows(1)
-    gather(0, 256)
+    turn_own()
+    gather(0, False)
     pl.when(even)(pass_prev)
-    pl.when(jnp.logical_not(even))(pass_next)
-    for there in (sib, (sib + 2) % 4, 9 - core):
-        arrived(there)
-
-    @pl.when(core == 1)
-    def _():
-        arrived(10, SHORT)
-
-    for i in range(2, WIN // 128):
-        turn_rows(i)
-    gather(256, WIN)
-
-    def product(q):
-        both = jnp.dot(o_main[q], g_hi[q], preferred_element_type=F32)
-        third = jnp.dot(o_main[q, :304], g_lo[q], preferred_element_type=F32)
-        return both[:304] + both[304:] + third + jnp.dot(o_left[q], g_last[q], preferred_element_type=F32)
-
-    acc[...] = product(0)
-
-    def multiply(q, _):
-        acc[...] += product(q)
-        return 0
-
-    lax.fori_loop(1, OFFS // 2, multiply, 0)
-
-    u = acc[:, 256:384]
-    u = u + pltpu.roll(u, 64, 1)
-    ufold[...] = u + pltpu.roll(u, 32, 1)
+    pl.when(odd)(pass_next)
+    pl.when(even)(took_next)
+    pl.when(odd)(took_prev)
+    gather(jnp.where(even, 1, 2), True)
+    pl.when(even)(took_prev)
+    pl.when(odd)(took_next)
+    gather(jnp.where(even, 2, 1), True)
+
+    def product(q, at):
+        both = jnp.dot(o_main[q], g_hi[q, :, at], preferred_element_type=F32)
+        third = jnp.dot(o_main[q, :304], g_lo[q, :, at], preferred_element_type=F32)
+        return both[:304] + both[304:] + third + jnp.dot(o_left[q], g_last[q, :, at], preferred_element_type=F32)
+
+    def multiply(ref, at, first, last):
+        def step(q, _):
+            ref[...] += product(q, at)
+            return 0
+
+        lax.fori_loop(first, last, step, 0)
+
+    main, side = slice(0, 256), slice(256, 384)
+    acc[...] = product(0, main)
+    multiply(acc, main, 1, OFFS // 2)
 
     def packed(half):
         v = ufold[pl.ds(pl.multiple_of(STEP * half, 8), 160), :]
@@ -297,26 +327,38 @@
 
     theirs = pl.ds(pl.multiple_of(STEP * (1 - core), 8), HALF)
     mine = pl.ds(pl.multiple_of(STEP * core, 8), HALF)
+    swap = [send(0, acc.at[theirs], ra, sibling), send(1, lpack, ral, sibling)]
+    cross = [send(2, q_ref.at[1 - chip], rq, beside), send(3, ql_ref, rql, beside)]
+    swap[0].start()
+    ufold[...] = product(0, side)
+    multiply(ufold, side, 1, 4)
+    swap[0].wait_recv()
+    q_ref[0] = acc[mine, :128] + ra[:, :128]
+    q_ref[1] = acc[mine, 128:] + ra[:, 128:]
+    cross[0].start()
+    multiply(ufold, side, 4, OFFS // 2)
+    u = ufold[...]
+    u = u + pltpu.roll(u, 64, 1)
+    ufold[...] = u + pltpu.roll(u, 32, 1)
     lpack[...] = packed(1 - core)
-    swap = [send(0, acc.at[theirs, pl.ds(0, 256)], ra, sibling), send(1, lpack, ral, sibling)]
-    for c in swap:
-        c.start()
+    swap[1].start()
     own_left = packed(core)
-    for c in swap:
-        c.wait_recv()
-    q0 = acc[mine, :128] + ra[:, :128]
-    q1 = acc[mine, 128:256] + ra[:, 128:]
+    hi, lo = split(jnp.concatenate([q_ref[0], q_ref[1]], axis=1))
+    edges = jnp.dot(hi, hot_send[:256], preferred_element_type=F32)
+    edges = edges + jnp.dot(lo, hot_send[:256], preferred_element_type=F32)
+    swap[1].wait_recv()
     ql = own_left + ral[...]
-    q_ref[0], q_ref[1], ql_ref[...] = q0, q1, ql
-
-    cross = [send(2, q_ref.at[1 - chip], rq, beside), send(3, ql_ref, rql, beside)]
-    for c in cross:
-        c.start()
-    hi, lo = split(jnp.concatenate([q0, q1, unpacked(ql)], axis=1))
-    edges = jnp.dot(hi, hot_send[...], preferred_element_type=F32) + jnp.dot(
-        lo, hot_send[...], preferred_element_type=F32
-    )
-    ht[0], ht[1] = edges[:, :128], edges[:, 128:]
+    ql_ref[...] = ql
+    cross[1].start()
+    hi, lo = split(unpacked(ql))
+    edges = edges + jnp.dot(hi, hot_send[256:], preferred_element_type=F32)
+    edges = edges + jnp.dot(lo, hot_send[256:], preferred_element_type=F32)
+    for i in range(2):
+        e = jnp.concatenate([edges[:, 128 * i : 128 * i + 128], jnp.zeros((8, 128), F32)], axis=0)
+        for a in range(3):
+            ht[i, 40 * a : 40 * a + 40] = e[40 * a : 40 * a + 40] + jnp.where(
+                lane_id >= EDGE, pltpu.roll(e[120:160], 96 - 32 * a, 1), 0.0
+            )
     heads = [send(4 + i, ht.at[0], hr.at[chip], peers[4 + i], 4 + chip) for i in range(2)]
     tails = send(6, ht.at[1], tr.at[chip], (up, core), 6 + chip)
     for c in (heads[1], tails, heads[0]):
@@ -342,7 +384,12 @@
     def _():
         tr[...] = jnp.zeros(tr.shape, F32)
 
-    hi, lo = split(jnp.concatenate([hr[0] + hr[1], tr[0] + tr[1]], axis=1))
+    def edge_rows(v):
+        thirds = [pltpu.roll(v[40 * a : 40 * a + 40], 32 * a + 32, 1) for a in range(3)]
+        quarter = jnp.where(lane_id < 32, thirds[0], jnp.where(lane_id < 64, thirds[1], thirds[2]))
+        return jnp.concatenate([v, quarter], axis=0)[:HALF]
+
+    hi, lo = split(jnp.concatenate([edge_rows(hr[0] + hr[1]), edge_rows(tr[0] + tr[1])], axis=1))
     moved = jnp.dot(hi, hot_recv[...], preferred_element_type=F32) + jnp.dot(
         lo, hot_recv[...], preferred_element_type=F32
     )
@@ -394,13 +441,13 @@
         pltpu.VMEM((OFFS, 304, F), F32),
         pltpu.VMEM((OFFS // 2, 608, 512), BF16),
         pltpu.VMEM((OFFS // 2, 304, 256), BF16),
-        pltpu.VMEM((592, WIN), BF16),
+        pltpu.VMEM((3, 592, 256), BF16),
         pltpu.VMEM((OFFS, 256), I32),
         pltpu.VMEM((2, 256), I32),
         pltpu.VMEM((OFFS // 2, 512, 384), BF16),
         pltpu.VMEM((OFFS // 2, 512, 384), BF16),
         pltpu.VMEM((OFFS // 2, 256, 384), BF16),
-        pltpu.VMEM((304, 384), F32),
+        pltpu.VMEM((304, 256), F32),
         pltpu.VMEM((304, 128), F32),
         pltpu.VMEM((384, 256), BF16),
         pltpu.VMEM((256, 256), BF16),
@@ -409,11 +456,11 @@
         pltpu.VMEM((40, 128), F32),
         pltpu.VMEM((2, HALF, 128), F32),
         pltpu.VMEM((40, 128), F32),
-        pltpu.VMEM((2, HALF, 128), F32),
+        pltpu.VMEM((2, 120, 128), F32),
         pltpu.VMEM((HALF, 128), F32),
         pltpu.VMEM((40, 128), F32),
-        pltpu.VMEM((2, HALF, 128), F32),
-        pltpu.VMEM((2, HALF, 128), F32),
+        pltpu.VMEM((2, 120, 128), F32),
+        pltpu.VMEM((2, 120, 128), F32),
         pltpu.VMEM((2, HALF, 128), F32),
         pltpu.VMEM((2, HALF, 128), F32),
         pltpu.VMEM((2, 384, 128), F32),

time: 53 us -> 56.2 us (1.060)
  Pallas kernels: 51.3 us -> 54.6 us
    pallas_call x1, Pallas kernels: 51.3 us -> 54.6 us  [body(): pl.pallas_call(kernel, out_shape=jax.ShapeDtypeStruct((ROWS, F), F32), in...]
where the time goes in v3:
time: 56.2 us; the launch traced here: 56.1 us
  Pallas kernels  54.6 us (97%)
  local copies, waits for them, and re-layouts  1.55 us (3%)
    pallas_call x1, Pallas kernels, body(): pl.pallas_call(kernel, out_shape=jax.ShapeDtypeStruct((ROWS, F), F32), in...  54.6 us
    unnamed x1, local copies, waits for them, and re-layouts  1.55 us

profile of v3, /device:TPU:1, one launch (start us, length us, event | category | flops | bytes accessed | tf_op | source)
XLA Modules:
  0.0 56.1 jit_solution(4249048015025307140)
XLA Ops:
  0.0 54.6 %translate.1 = f32[72,296]{1,0:T(8,128)} custom-call(f32[72,296]{1,0:T(8,128)} %den_hbm.1, f32[16,296,296]{2,1,0:T(8,128)} %ops.1, s32[1,128]{1,0:T(1,128)} %bitcast.2, s32[1,128]{1,0:T(1,128)} %bitcast.3, s32[1,16,288]{2,1,0:T(8,128)} %tgt_hbm.1, s32[1,16,288]{2,1,0:T(8,128)} %src_hbm.1), custom_call_target="tpu_custom_call" | custom-call | tf_op jit(solution)/shard_map/translate/pallas_call | solution.py:476
  54.6 1.5 %copy.8 = f32[72,296]{1,0:T(8,128)} copy(f32[72,296]{1,0:T(8,128)} %translate.1) | data formatting | bytes 170496

commit v4 on v3

--- a/solution.py
+++ b/solution.py
@@ -42,7 +42,7 @@
 
 def kernel(
     den_hbm, ops, ocnt_hbm, gcnt_hbm, tgt_hbm, src_hbm, out,
-    den, ocnt, gcnt, tgt, src, rx, stage, o_main, o_left, xt, pmain, pleft, g_hi, g_lo, g_last, acc, ufold,
+    den, ocnt, gcnt, tgt, src, rx, stage, o_main, o_left, xt, pmain, pleft, g_both, g_lo, g_last, acc, side, ufold,
     hot_send, hot_recv, lpack, ra, ral, q_ref, ql_ref, ht, rq, rql, hr, tr, v_ref, fr, fin, tt,
     in_sem, op_sem, ici_send, sib_send, rsem, osend, orecv,
 ):
@@ -93,18 +93,14 @@
     turn = jnp.where(j == slot_of_column(iota((CAP, 384), 1)), 1.0, 0.0).astype(F32)
     turned = jnp.dot(place.astype(F32), turn, precision=lax.Precision.HIGHEST, preferred_element_type=F32)
     turned = (turned + 0.25 * jnp.where(turned < 0, -1.0, 1.0)).astype(I32)
-    pmain[...] = turned[:, :256]
     lane_id = iota((1, 128), 1)
     group_of_lane = lane_id >> 5
-    for t in range(2):
-        rows = []
-        for h in range(2):
-            row = jnp.zeros((1, 128), I32)
-            for a in range(4):
-                k = 8 * t + 4 * h + a
-                row = jnp.where(group_of_lane == a, turned[k : k + 1, 256:384], row)
-            rows.append(row)
-        pleft[t : t + 1] = jnp.concatenate(rows, axis=1)
+    for i in range(4):
+        pmain[i : i + 1] = jnp.concatenate([turned[k : k + 1, :256] for k in range(4 * i, 4 * i + 4)], axis=1)
+        row = jnp.zeros((1, 128), I32)
+        for a in range(4):
+            row = jnp.where(group_of_lane == a, turned[4 * i + a : 4 * i + a + 1, 256:384], row)
+        pleft[:, 128 * i : 128 * i + 128] = row
 
     s = slot_of_column(iota((384, 128), 0))
     real = iota((384, 128), 0) < CAP
@@ -153,18 +149,18 @@
 
     stage[:, pl.ds(F, 8), :] = jnp.zeros((OFFS, 8, F), F32)
 
-    def split_pair(q, _):
-        for par in range(2):
-            k = 2 * q + par
+    def split_eight(q, _):
+        for a in range(8):
+            k = 8 * q + a
             op_copy(k).wait()
             v = stage[k]
             hi = v.astype(BF16)
             hi32 = hi.astype(F32)
             lo32 = v - hi32
-            o_main[q, :304, 256 * par : 256 * par + 256] = hi[:, :256]
-            o_main[q, 304:, 256 * par : 256 * par + 256] = lo32[:, :256].astype(BF16)
+            o_main[q, :304, 256 * a : 256 * a + 256] = hi[:, :256]
+            o_main[q, 304:, 256 * a : 256 * a + 256] = lo32[:, :256].astype(BF16)
             last = jnp.concatenate([hi32[:, 256:], hi32[:, 256:], lo32[:, 256:], jnp.zeros((304, 8), F32)], axis=1)
-            o_left[q, :, 128 * par : 128 * par + 128] = last.astype(BF16)
+            o_left[q, :, 128 * a : 128 * a + 128] = last.astype(BF16)
         return 0
 
     def arrived(there, count=TILES):
@@ -226,87 +222,73 @@
         turn_rows(2, 1, [wide_left(*a) for a in row_tiles(0, range(16, 32))])
 
     def gathered(row, t):
-        hot = jnp.where(iota((256, 256), 0) + 256 * t == row, 1.0, 0.0).astype(BF16)
-        return jnp.dot(xt[t], hot, preferred_element_type=F32)
-
-    def put(q, par, columns, g, add):
+        rows = xt[0] if t == 0 else jnp.concatenate([xt[1], xt[2]], axis=1)
+        hot = jnp.where(iota((rows.shape[1], row.shape[1]), 0) + 256 * t == row, 1.0, 0.0).astype(BF16)
+        return jnp.dot(rows, hot, preferred_element_type=F32)
+
+    def put(q, a, g, left, add):
         tail = jnp.concatenate([g[512:592], g[512:552], jnp.zeros((8, g.shape[1]), F32)], axis=0)
-        for ref, at, v in (
-            (g_hi, pl.ds(256 * par, 256), g[:256]),
-            (g_lo, pl.ds(256 * par, 256), g[256:512]),
-            (g_last, pl.ds(128 * par, 128), tail),
+        rows, short = pl.ds(256 * a, 256), pl.ds(128 * a, 128)
+        for ref, at, columns, v in (
+            (g_both, rows, pl.ds(256, 128) if left else pl.ds(0, 256), g[:256]),
+            (g_both, rows, pl.ds(384, 128), g[256:512]) if left else (g_lo, rows, pl.ds(0, 256), g[256:512]),
+            (g_last, short, pl.ds(256, 128) if left else pl.ds(0, 256), tail),
         ):
             v = v.astype(BF16)
             ref[q, at, columns] = ref[q, at, columns] + v if add else v
 
     def gather(t, add):
-        def gather_pair(q, _):
-            for par in range(2):
-                put(q, par, pl.ds(0, 256), gathered(pmain[pl.ds(2 * q + par, 1), :], t), add)
+        def gather_eight(q, _):
+            for h in range(2):
+                g = gathered(pmain[pl.ds(2 * q + h, 1), :], t)
+                for a in range(4):
+                    put(q, 4 * h + a, g[:, 256 * a : 256 * a + 256], False, add)
             return 0
 
-        lax.fori_loop(0, OFFS // 2, gather_pair, 0)
-
-        def gather_left(i, _):
-            g = gathered(pleft[pl.ds(i, 1), :], t)
-            for kk in range(8):
-                h, a = kk // 4, kk % 4
-                part = jnp.where(group_of_lane == a, g[:, 128 * h : 128 * h + 128], 0.0)
-                put(4 * i + kk // 2, kk % 2, pl.ds(256, 128), part, add)
-            return 0
-
-        lax.fori_loop(0, 2, gather_left, 0)
-
-    lax.fori_loop(0, OFFS // 4, split_pair, 0)
+        lax.fori_loop(0, 2, gather_eight, 0)
+        g = gathered(pleft[...], t)
+        for k in range(OFFS):
+            part = g[:, 128 * (k // 4) : 128 * (k // 4) + 128]
+            put(k // 8, k % 8, jnp.where(group_of_lane == k % 4, part, 0.0), True, add)
+
+    lax.fori_loop(0, 1, split_eight, 0)
     pass_own()
-    lax.fori_loop(OFFS // 4, OFFS // 2, split_pair, 0)
+    lax.fori_loop(1, 2, split_eight, 0)
     even = b % 2 == 0
     pl.when(even)(pass_next)
     odd = jnp.logical_not(even)
     pl.when(odd)(pass_prev)
 
-    def took_prev():
-        arrived(sib)
-        arrived((sib + 2) % 4)
-        turn_prev()
-
-    def took_next():
-        arrived(9 - core)
-
-        @pl.when(core == 1)
-        def _():
-            arrived(10, SHORT)
-
-        turn_next()
-
+    pl.when(even)(pass_prev)
+    pl.when(odd)(pass_next)
     arrived(4 + sib)
     arrived(4 + (sib + 2) % 4)
     turn_own()
     gather(0, False)
-    pl.when(even)(pass_prev)
-    pl.when(odd)(pass_next)
-    pl.when(even)(took_next)
-    pl.when(odd)(took_prev)
-    gather(jnp.where(even, 1, 2), True)
-    pl.when(even)(took_prev)
-    pl.when(odd)(took_next)
-    gather(jnp.where(even, 2, 1), True)
-
-    def product(q, at):
-        both = jnp.dot(o_main[q], g_hi[q, :, at], preferred_element_type=F32)
-        third = jnp.dot(o_main[q, :304], g_lo[q, :, at], preferred_element_type=F32)
-        return both[:304] + both[304:] + third + jnp.dot(o_left[q], g_last[q, :, at], preferred_element_type=F32)
-
-    def multiply(ref, at, first, last):
-        def step(q, _):
-            ref[...] += product(q, at)
-            return 0
-
-        lax.fori_loop(first, last, step, 0)
-
-    main, side = slice(0, 256), slice(256, 384)
-    acc[...] = product(0, main)
-    multiply(acc, main, 1, OFFS // 2)
+    for there in (sib, (sib + 2) % 4, 9 - core):
+        arrived(there)
+
+    @pl.when(core == 1)
+    def _():
+        arrived(10, SHORT)
+
+    turn_next()
+    turn_prev()
+    gather(1, True)
+
+    acc[...] = jnp.zeros(acc.shape, F32)
+    side[...] = jnp.zeros(side.shape, F32)
+
+    def multiply(q, _):
+        both = jnp.dot(o_main[q], g_both[q], preferred_element_type=F32)
+        third = jnp.dot(o_main[q, :304], g_lo[q], preferred_element_type=F32)
+        last = jnp.dot(o_left[q], g_last[q], preferred_element_type=F32)
+        both = both[:304] + both[304:]
+        acc[...] += both[:, :256] + third + last[:, :256]
+        side[...] += both[:, 256:384] + both[:, 384:] + last[:, 256:]
+        return 0
+
+    lax.fori_loop(0, 2, multiply, 0)
 
     def packed(half):
         v = ufold[pl.ds(pl.multiple_of(STEP * half, 8), 160), :]
@@ -328,31 +310,25 @@
     theirs = pl.ds(pl.multiple_of(STEP * (1 - core), 8), HALF)
     mine = pl.ds(pl.multiple_of(STEP * core, 8), HALF)
     swap = [send(0, acc.at[theirs], ra, sibling), send(1, lpack, ral, sibling)]
-    cross = [send(2, q_ref.at[1 - chip], rq, beside), send(3, ql_ref, rql, beside)]
     swap[0].start()
-    ufold[...] = product(0, side)
-    multiply(ufold, side, 1, 4)
-    swap[0].wait_recv()
-    q_ref[0] = acc[mine, :128] + ra[:, :128]
-    q_ref[1] = acc[mine, 128:] + ra[:, 128:]
-    cross[0].start()
-    multiply(ufold, side, 4, OFFS // 2)
-    u = ufold[...]
+    u = side[...]
     u = u + pltpu.roll(u, 64, 1)
     ufold[...] = u + pltpu.roll(u, 32, 1)
     lpack[...] = packed(1 - core)
     swap[1].start()
     own_left = packed(core)
-    hi, lo = split(jnp.concatenate([q_ref[0], q_ref[1]], axis=1))
-    edges = jnp.dot(hi, hot_send[:256], preferred_element_type=F32)
-    edges = edges + jnp.dot(lo, hot_send[:256], preferred_element_type=F32)
-    swap[1].wait_recv()
+    for c in swap:
+        c.wait_recv()
+    q0 = acc[mine, :128] + ra[:, :128]
+    q1 = acc[mine, 128:256] + ra[:, 128:]
     ql = own_left + ral[...]
-    ql_ref[...] = ql
-    cross[1].start()
-    hi, lo = split(unpacked(ql))
-    edges = edges + jnp.dot(hi, hot_send[256:], preferred_element_type=F32)
-    edges = edges + jnp.dot(lo, hot_send[256:], preferred_element_type=F32)
+    q_ref[0], q_ref[1], ql_ref[...] = q0, q1, ql
+    cross = [send(2, q_ref.at[1 - chip], rq, beside), send(3, ql_ref, rql, beside)]
+    for c in cross:
+        c.start()
+    hi, lo = split(jnp.concatenate([q0, q1, unpacked(ql)], axis=1))
+    edges = jnp.dot(hi, hot_send[...], preferred_element_type=F32)
+    edges = edges + jnp.dot(lo, hot_send[...], preferred_element_type=F32)
     for i in range(2):
         e = jnp.concatenate([edges[:, 128 * i : 128 * i + 128], jnp.zeros((8, 128), F32)], axis=0)
         for a in range(3):
@@ -439,15 +415,16 @@
         pltpu.VMEM((1, OFFS, CAP), I32),
         pltpu.VMEM((12, TILES, 8, 128), F32),
         pltpu.VMEM((OFFS, 304, F), F32),
-        pltpu.VMEM((OFFS // 2, 608, 512), BF16),
-        pltpu.VMEM((OFFS // 2, 304, 256), BF16),
+        pltpu.VMEM((2, 608, 2048), BF16),
+        pltpu.VMEM((2, 304, 1024), BF16),
         pltpu.VMEM((3, 592, 256), BF16),
-        pltpu.VMEM((OFFS, 256), I32),
-        pltpu.VMEM((2, 256), I32),
-        pltpu.VMEM((OFFS // 2, 512, 384), BF16),
-        pltpu.VMEM((OFFS // 2, 512, 384), BF16),
-        pltpu.VMEM((OFFS // 2, 256, 384), BF16),
+        pltpu.VMEM((4, 1024), I32),
+        pltpu.VMEM((1, 512), I32),
+        pltpu.VMEM((2, 2048, 512), BF16),
+        pltpu.VMEM((2, 2048, 256), BF16),
+        pltpu.VMEM((2, 1024, 384), BF16),
         pltpu.VMEM((304, 256), F32),
+        pltpu.VMEM((304, 128), F32),
         pltpu.VMEM((304, 128), F32),
         pltpu.VMEM((384, 256), BF16),
         pltpu.VMEM((256, 256), BF16),

time: 56.2 us -> 49 us (0.87)
  Pallas kernels: 54.6 us -> 47.3 us
    pallas_call x1, Pallas kernels: 54.6 us -> 47.3 us  [body(): pl.pallas_call(kernel, out_shape=jax.ShapeDtypeStruct((ROWS, F), F32), in...]
where the time goes in v4:
time: 49 us; the launch traced here: 48.9 us
  Pallas kernels  47.3 us (97%)
  local copies, waits for them, and re-layouts  1.55 us (3%)
    pallas_call x1, Pallas kernels, body(): pl.pallas_call(kernel, out_shape=jax.ShapeDtypeStruct((ROWS, F), F32), in...  47.3 us
    unnamed x1, local copies, waits for them, and re-layouts  1.55 us

profile of v4, /device:TPU:1, one launch (start us, length us, event | category | flops | bytes accessed | tf_op | source)
XLA Modules:
  0.0 48.9 jit_solution(9049100553666578636)
XLA Ops:
  0.0 47.3 %translate.1 = f32[72,296]{1,0:T(8,128)} custom-call(f32[72,296]{1,0:T(8,128)} %den_hbm.1, f32[16,296,296]{2,1,0:T(8,128)} %ops.1, s32[1,128]{1,0:T(1,128)} %bitcast.2, s32[1,128]{1,0:T(1,128)} %bitcast.3, s32[1,16,288]{2,1,0:T(8,128)} %tgt_hbm.1, s32[1,16,288]{2,1,0:T(8,128)} %src_hbm.1), custom_call_target="tpu_custom_call" | custom-call | tf_op jit(solution)/shard_map/translate/pallas_call | solution.py:453
  47.3 1.5 %copy.8 = f32[72,296]{1,0:T(8,128)} copy(f32[72,296]{1,0:T(8,128)} %translate.1) | data formatting | bytes 170496

commit v5 on v4

--- a/solution.py
+++ b/solution.py
@@ -43,7 +43,7 @@
 def kernel(
     den_hbm, ops, ocnt_hbm, gcnt_hbm, tgt_hbm, src_hbm, out,
     den, ocnt, gcnt, tgt, src, rx, stage, o_main, o_left, xt, pmain, pleft, g_both, g_lo, g_last, acc, side, ufold,
-    hot_send, hot_recv, lpack, ra, ral, q_ref, ql_ref, ht, rq, rql, hr, tr, v_ref, fr, fin, tt,
+    hot_send, hot_recv, lpack, ra, ral, q_ref, ql_ref, ht, rq, rql, hr, tr, qh, qt, v_ref, fr, fin, tt,
     in_sem, op_sem, ici_send, sib_send, rsem, osend, orecv,
 ):
     b, o = lax.axis_index("box"), lax.axis_index("op")
@@ -102,20 +102,26 @@
             row = jnp.where(group_of_lane == a, turned[4 * i + a : 4 * i + a + 1, 256:384], row)
         pleft[:, 128 * i : 128 * i + 128] = row
 
-    s = slot_of_column(iota((384, 128), 0))
-    real = iota((384, 128), 0) < CAP
-    lane = iota((384, 128), 1)
-    is_head = real & (s >= CAP - EDGE) & (os1 + s - CAP >= gs1) & (s - (CAP - EDGE) == lane)
+    s = slot_of_column(iota((256, 128), 0))
+    lane = iota((256, 128), 1)
+    is_head = (s >= CAP - EDGE) & (os1 + s - CAP >= gs1) & (s - (CAP - EDGE) == lane)
     box1 = os1 + s
     tail = jnp.where((box1 >= os2) & (box1 < gs2), box1 - os2, jnp.where(box1 + CAP < gs2, box1 + CAP - os2, -1))
     hot_send[:, :128] = jnp.where(is_head, 1.0, 0.0).astype(BF16)
-    hot_send[:, 128:] = jnp.where(real & (tail == lane), 1.0, 0.0).astype(BF16)
-    r = iota((256, 128), 0)
-    slot = jnp.where(r < 128, os2 - os1 + r - EDGE, r - 128)
-    known = jnp.where(r < 128, r, r - 128) < EDGE
-    lane = iota((256, 128), 1)
-    hot_recv[:, :128] = jnp.where(known & (slot == slot_of_column(lane + 128 * chip)), 1.0, 0.0).astype(BF16)
-    hot_recv[:, 128:] = jnp.where(known & (lane < 32) & (slot == slot_of_column(lane + 256)), 1.0, 0.0).astype(BF16)
+    hot_send[:, 128:] = jnp.where(tail == lane, 1.0, 0.0).astype(BF16)
+    r = iota((512, 128), 0)
+    c = r & 127
+    s = slot_of_column(256 + (c & 31))
+    head = jnp.where((s >= CAP - EDGE) & (os2 + s - CAP >= gs2), os2 - os1 + s - CAP, -1)
+    box0 = os0 + s
+    tail = jnp.where((box0 >= os1) & (box0 < gs1), box0, jnp.where(box0 + CAP < gs1, box0 + CAP, -1))
+    tail = jnp.where(tail >= 0, tail - os1, -1)
+    far_slot = jnp.where(c < 32, jnp.where(r < 384, head, tail), -1)
+    near_slot = jnp.where(c < EDGE, jnp.where(r < 128, os2 - os1 + c - EDGE, c), -1)
+    slot = jnp.where(r < 256, near_slot, far_slot)
+    lane = iota((512, 128), 1)
+    hot_recv[:, :128] = jnp.where(slot == slot_of_column(lane + 128 * chip), 1.0, 0.0).astype(BF16)
+    hot_recv[:, 128:] = jnp.where((lane < 32) & (slot == slot_of_column(lane + 256)), 1.0, 0.0).astype(BF16)
 
     def block_copy(here, there, count, send, device):
         return pltpu.make_async_remote_copy(
@@ -279,16 +285,21 @@
     acc[...] = jnp.zeros(acc.shape, F32)
     side[...] = jnp.zeros(side.shape, F32)
 
-    def multiply(q, _):
-        both = jnp.dot(o_main[q], g_both[q], preferred_element_type=F32)
+    def multiply_main(q, _):
+        both = jnp.dot(o_main[q], g_both[q, :, :256], preferred_element_type=F32)
         third = jnp.dot(o_main[q, :304], g_lo[q], preferred_element_type=F32)
-        last = jnp.dot(o_left[q], g_last[q], preferred_element_type=F32)
+        last = jnp.dot(o_left[q], g_last[q, :, :256], preferred_element_type=F32)
+        acc[...] += both[:304] + both[304:] + third + last
+        return 0
+
+    def multiply_side(q, _):
+        both = jnp.dot(o_main[q], g_both[q, :, 256:], preferred_element_type=F32)
+        last = jnp.dot(o_left[q], g_last[q, :, 256:], preferred_element_type=F32)
         both = both[:304] + both[304:]
-        acc[...] += both[:, :256] + third + last[:, :256]
-        side[...] += both[:, 256:384] + both[:, 384:] + last[:, 256:]
+        side[...] += both[:, :128] + both[:, 128:] + last
         return 0
 
-    lax.fori_loop(0, 2, multiply, 0)
+    lax.fori_loop(0, 2, multiply_main, 0)
 
     def packed(half):
         v = ufold[pl.ds(pl.multiple_of(STEP * half, 8), 160), :]
@@ -311,22 +322,12 @@
     mine = pl.ds(pl.multiple_of(STEP * core, 8), HALF)
     swap = [send(0, acc.at[theirs], ra, sibling), send(1, lpack, ral, sibling)]
     swap[0].start()
-    u = side[...]
-    u = u + pltpu.roll(u, 64, 1)
-    ufold[...] = u + pltpu.roll(u, 32, 1)
-    lpack[...] = packed(1 - core)
-    swap[1].start()
-    own_left = packed(core)
-    for c in swap:
-        c.wait_recv()
+    lax.fori_loop(0, 1, multiply_side, 0)
+    swap[0].wait_recv()
     q0 = acc[mine, :128] + ra[:, :128]
     q1 = acc[mine, 128:256] + ra[:, 128:]
-    ql = own_left + ral[...]
-    q_ref[0], q_ref[1], ql_ref[...] = q0, q1, ql
-    cross = [send(2, q_ref.at[1 - chip], rq, beside), send(3, ql_ref, rql, beside)]
-    for c in cross:
-        c.start()
-    hi, lo = split(jnp.concatenate([q0, q1, unpacked(ql)], axis=1))
+    q_ref[0], q_ref[1] = q0, q1
+    hi, lo = split(jnp.concatenate([q0, q1], axis=1))
     edges = jnp.dot(hi, hot_send[...], preferred_element_type=F32)
     edges = edges + jnp.dot(lo, hot_send[...], preferred_element_type=F32)
     for i in range(2):
@@ -337,7 +338,21 @@
             )
     heads = [send(4 + i, ht.at[0], hr.at[chip], peers[4 + i], 4 + chip) for i in range(2)]
     tails = send(6, ht.at[1], tr.at[chip], (up, core), 6 + chip)
-    for c in (heads[1], tails, heads[0]):
+    cross = [send(2, q_ref.at[1 - chip], rq, beside), send(3, ql_ref, rql, beside)]
+    for c in (heads[1], tails, heads[0], cross[0]):
+        c.start()
+    lax.fori_loop(1, 2, multiply_side, 0)
+    u = side[...]
+    u = u + pltpu.roll(u, 64, 1)
+    ufold[...] = u + pltpu.roll(u, 32, 1)
+    lpack[...] = packed(1 - core)
+    swap[1].start()
+    own_left = packed(core)
+    swap[1].wait_recv()
+    ql_ref[...] = own_left + ral[...]
+    head_ql = [send(9 + i, ql_ref, qh.at[chip], peers[4 + i], 9 + chip) for i in range(2)]
+    tail_ql = send(11, ql_ref, qt.at[chip], (up, core), 11 + chip)
+    for c in (head_ql[1], tail_ql, head_ql[0], cross[1]):
         c.start()
     for c in cross:
         c.wait_recv()
@@ -350,22 +365,26 @@
     own_left = unpacked(jnp.where(keep, ql_ref[...] + rql[...], 0.0))
     for i in range(2):
         send(4 + i, ht.at[0], hr.at[i], peers[4], 4 + i).wait_recv()
+        send(9, ql_ref, qh.at[i], peers[4], 9 + i).wait_recv()
 
     @pl.when(chip == 0)
     def _():
         for i in range(2):
             send(6, ht.at[1], tr.at[i], peers[4], 6 + i).wait_recv()
+            send(11, ql_ref, qt.at[i], peers[4], 11 + i).wait_recv()
 
     @pl.when(chip == 1)
     def _():
         tr[...] = jnp.zeros(tr.shape, F32)
+        qt[...] = jnp.zeros(qt.shape, F32)
 
     def edge_rows(v):
         thirds = [pltpu.roll(v[40 * a : 40 * a + 40], 32 * a + 32, 1) for a in range(3)]
         quarter = jnp.where(lane_id < 32, thirds[0], jnp.where(lane_id < 64, thirds[1], thirds[2]))
         return jnp.concatenate([v, quarter], axis=0)[:HALF]
 
-    hi, lo = split(jnp.concatenate([edge_rows(hr[0] + hr[1]), edge_rows(tr[0] + tr[1])], axis=1))
+    near = [edge_rows(v[0] + v[1]) for v in (hr, tr)]
+    hi, lo = split(jnp.concatenate([*near, unpacked(qh[0] + qh[1]), unpacked(qt[0] + qt[1])], axis=1))
     moved = jnp.dot(hi, hot_recv[...], preferred_element_type=F32) + jnp.dot(
         lo, hot_recv[...], preferred_element_type=F32
     )
@@ -401,7 +420,7 @@
         for i in range(2):
             to_next_segment(i, SHORT).wait_send()
 
-    for c in (*swap, *cross, *heads, tails, last):
+    for c in (*swap, *cross, *heads, tails, *head_ql, tail_ql, last):
         c.wait_send()
 
 
@@ -426,8 +445,8 @@
         pltpu.VMEM((304, 256), F32),
         pltpu.VMEM((304, 128), F32),
         pltpu.VMEM((304, 128), F32),
-        pltpu.VMEM((384, 256), BF16),
         pltpu.VMEM((256, 256), BF16),
+        pltpu.VMEM((512, 256), BF16),
         pltpu.VMEM((40, 128), F32),
         pltpu.VMEM((HALF, 256), F32),
         pltpu.VMEM((40, 128), F32),
@@ -438,6 +457,8 @@
         pltpu.VMEM((40, 128), F32),
         pltpu.VMEM((2, 120, 128), F32),
         pltpu.VMEM((2, 120, 128), F32),
+        pltpu.VMEM((2, 40, 128), F32),
+        pltpu.VMEM((2, 40, 128), F32),
         pltpu.VMEM((2, HALF, 128), F32),
         pltpu.VMEM((2, HALF, 128), F32),
         pltpu.VMEM((2, 384, 128), F32),
@@ -447,8 +468,8 @@
         pltpu.SemaphoreType.DMA((5,)),
         pltpu.SemaphoreType.DMA((6,)),
         pltpu.SemaphoreType.DMA((12,)),
-        pltpu.SemaphoreType.DMA((9,)),
-        pltpu.SemaphoreType.DMA((9,)),
+        pltpu.SemaphoreType.DMA((12,)),
+        pltpu.SemaphoreType.DMA((13,)),
     ]
     return pl.pallas_call(
         kernel,

time: 49 us -> 49.6 us (1.012)
  Pallas kernels: 47.3 us -> 48 us
    pallas_call x1, Pallas kernels: 47.3 us -> 48 us  [body(): pl.pallas_call(kernel, out_shape=jax.ShapeDtypeStruct((ROWS, F), F32), in...]
where the time goes in v5:
time: 49.6 us; the launch traced here: 49.5 us
  Pallas kernels  48 us (97%)
  local copies, waits for them, and re-layouts  1.55 us (3%)
    pallas_call x1, Pallas kernels, body(): pl.pallas_call(kernel, out_shape=jax.ShapeDtypeStruct((ROWS, F), F32), in...  48 us
    unnamed x1, local copies, waits for them, and re-layouts  1.55 us

profile of v5, /device:TPU:1, one launch (start us, length us, event | category | flops | bytes accessed | tf_op | source)
XLA Modules:
  0.0 49.5 jit_solution(5150381863737901079)
XLA Ops:
  0.0 48.0 %translate.1 = f32[72,296]{1,0:T(8,128)} custom-call(f32[72,296]{1,0:T(8,128)} %den_hbm.1, f32[16,296,296]{2,1,0:T(8,128)} %ops.1, s32[1,128]{1,0:T(1,128)} %bitcast.2, s32[1,128]{1,0:T(1,128)} %bitcast.3, s32[1,16,288]{2,1,0:T(8,128)} %tgt_hbm.1, s32[1,16,288]{2,1,0:T(8,128)} %src_hbm.1), custom_call_target="tpu_custom_call" | custom-call | tf_op jit(solution)/shard_map/translate/pallas_call | solution.py:474
  48.0 1.5 %copy.8 = f32[72,296]{1,0:T(8,128)} copy(f32[72,296]{1,0:T(8,128)} %translate.1) | data formatting | bytes 170496

commit v6 on v5

--- a/solution.py
+++ b/solution.py
@@ -53,13 +53,21 @@
     up, down = (b + 1) % n, (b + n - 1) % n
     sibling, beside = (b, sib), (b, far)
     peers = [sibling, beside, (up, o), (up, far), (down, o), (down, far)]
+    has_down, has_up = b > 0, b < n - 1
 
     def op_copy(k):
         return pltpu.make_async_copy(ops.at[k], stage.at[k, pl.ds(0, F)], op_sem.at[k])
 
     barrier = pltpu.get_barrier_semaphore()
-    for peer in peers:
-        pl.semaphore_signal(barrier, inc=1, device_id=peer, device_id_type=MESH)
+
+
+    def greet(some):
+        for peer in some:
+            pl.semaphore_signal(barrier, inc=1, device_id=peer, device_id_type=MESH)
+
+    greet(peers[:2])
+    pl.when(has_up)(lambda: greet(peers[2:4]))
+    pl.when(has_down)(lambda: greet(peers[4:]))
     pairs = ((den_hbm, den), (ocnt_hbm, ocnt), (gcnt_hbm, gcnt), (tgt_hbm, tgt), (src_hbm, src))
     inputs = [pltpu.make_async_copy(a, v, in_sem.at[i]) for i, (a, v) in enumerate(pairs)]
     for c in inputs:
@@ -129,7 +137,7 @@
             send_sem=send, recv_sem=rsem.at[there], device_id=device, device_id_type=MESH,
         )
 
-    pl.semaphore_wait(barrier, len(peers))
+    pl.semaphore_wait(barrier, jnp.where(has_up & has_down, 6, 4))
 
     def to_prev_segment(i):
         return block_copy(me, o, TILES, ici_send.at[1 + i], peers[2 + i])
@@ -140,13 +148,16 @@
     to_beside = block_copy(me, me, TILES, ici_send.at[0], beside)
     to_sibling = block_copy(me, me, TILES, sib_send.at[0], sibling)
     for i in (1, 0):
-        to_prev_segment(i).start()
-
-        @pl.when(o < 2)
+
+        @pl.when(has_up)
+        def _():
+            to_prev_segment(i).start()
+
+        @pl.when(has_down & (o < 2))
         def _():
             to_next_segment(i, TILES).start()
 
-        @pl.when(o == 2)
+        @pl.when(has_down & (o == 2))
         def _():
             to_next_segment(i, SHORT).start()
 
@@ -243,7 +254,7 @@
             v = v.astype(BF16)
             ref[q, at, columns] = ref[q, at, columns] + v if add else v
 
-    def gather(t, add):
+    def gather_main(t, add):
         def gather_eight(q, _):
             for h in range(2):
                 g = gathered(pmain[pl.ds(2 * q + h, 1), :], t)
@@ -252,35 +263,52 @@
             return 0
 
         lax.fori_loop(0, 2, gather_eight, 0)
+
+    def gather_left(t, add):
         g = gathered(pleft[...], t)
         for k in range(OFFS):
             part = g[:, 128 * (k // 4) : 128 * (k // 4) + 128]
             put(k // 8, k % 8, jnp.where(group_of_lane == k % 4, part, 0.0), True, add)
 
+    @pl.when(jnp.logical_not(has_down))
+    def _():
+        rx[0:4] = jnp.zeros((4, TILES, 8, 128), F32)
+
+    @pl.when(jnp.logical_not(has_up))
+    def _():
+        rx[8:11] = jnp.zeros((3, TILES, 8, 128), F32)
+
     lax.fori_loop(0, 1, split_eight, 0)
     pass_own()
     lax.fori_loop(1, 2, split_eight, 0)
     even = b % 2 == 0
-    pl.when(even)(pass_next)
     odd = jnp.logical_not(even)
-    pl.when(odd)(pass_prev)
-
-    pl.when(even)(pass_prev)
-    pl.when(odd)(pass_next)
+    pl.when(even & has_up)(pass_next)
+    pl.when(odd & has_down)(pass_prev)
+    pl.when(even & has_down)(pass_prev)
+    pl.when(odd & has_up)(pass_next)
     arrived(4 + sib)
     arrived(4 + (sib + 2) % 4)
     turn_own()
-    gather(0, False)
-    for there in (sib, (sib + 2) % 4, 9 - core):
-        arrived(there)
-
-    @pl.when(core == 1)
+    gather_main(0, False)
+    gather_left(0, False)
+
+    @pl.when(has_down)
+    def _():
+        arrived(sib)
+        arrived((sib + 2) % 4)
+
+    @pl.when(has_up)
+    def _():
+        arrived(9 - core)
+
+    @pl.when(has_up & (core == 1))
     def _():
         arrived(10, SHORT)
 
     turn_next()
     turn_prev()
-    gather(1, True)
+    gather_main(1, True)
 
     acc[...] = jnp.zeros(acc.shape, F32)
     side[...] = jnp.zeros(side.shape, F32)
@@ -322,7 +350,7 @@
     mine = pl.ds(pl.multiple_of(STEP * core, 8), HALF)
     swap = [send(0, acc.at[theirs], ra, sibling), send(1, lpack, ral, sibling)]
     swap[0].start()
-    lax.fori_loop(0, 1, multiply_side, 0)
+    gather_left(1, True)
     swap[0].wait_recv()
     q0 = acc[mine, :128] + ra[:, :128]
     q1 = acc[mine, 128:256] + ra[:, 128:]
@@ -339,9 +367,20 @@
     heads = [send(4 + i, ht.at[0], hr.at[chip], peers[4 + i], 4 + chip) for i in range(2)]
     tails = send(6, ht.at[1], tr.at[chip], (up, core), 6 + chip)
     cross = [send(2, q_ref.at[1 - chip], rq, beside), send(3, ql_ref, rql, beside)]
-    for c in (heads[1], tails, heads[0], cross[0]):
-        c.start()
-    lax.fori_loop(1, 2, multiply_side, 0)
+
+    def with_up(name, *copies):
+        for c in copies:
+            pl.when(has_up)(c.start if name == "start" else c.wait_send)
+
+    def with_down(name, *copies):
+        for c in copies:
+            pl.when(has_down)(c.start if name == "start" else c.wait_send)
+
+    with_down("start", heads[1])
+    with_up("start", tails)
+    with_down("start", heads[0])
+    cross[0].start()
+    lax.fori_loop(0, 2, multiply_side, 0)
     u = side[...]
     u = u + pltpu.roll(u, 64, 1)
     ufold[...] = u + pltpu.roll(u, 32, 1)
@@ -352,8 +391,10 @@
     ql_ref[...] = own_left + ral[...]
     head_ql = [send(9 + i, ql_ref, qh.at[chip], peers[4 + i], 9 + chip) for i in range(2)]
     tail_ql = send(11, ql_ref, qt.at[chip], (up, core), 11 + chip)
-    for c in (head_ql[1], tail_ql, head_ql[0], cross[1]):
-        c.start()
+    with_down("start", head_ql[1])
+    with_up("start", tail_ql)
+    with_down("start", head_ql[0])
+    cross[1].start()
     for c in cross:
         c.wait_recv()
     s = slot_of_column(iota((1, 128), 1) + 128 * chip)
@@ -363,17 +404,26 @@
     box1 = os1 + slot_of_column(256 + (iota((1, 128), 1) & 31))
     keep = (box1 >= gs1) & (box1 < gs2) & (box1 < os2)
     own_left = unpacked(jnp.where(keep, ql_ref[...] + rql[...], 0.0))
-    for i in range(2):
-        send(4 + i, ht.at[0], hr.at[i], peers[4], 4 + i).wait_recv()
-        send(9, ql_ref, qh.at[i], peers[4], 9 + i).wait_recv()
-
-    @pl.when(chip == 0)
+    @pl.when(has_up)
+    def _():
+        for i in range(2):
+            send(4 + i, ht.at[0], hr.at[i], peers[4], 4 + i).wait_recv()
+            send(9, ql_ref, qh.at[i], peers[4], 9 + i).wait_recv()
+
+    @pl.when(jnp.logical_not(has_up))
+    def _():
+        hr[...] = jnp.zeros(hr.shape, F32)
+        qh[...] = jnp.zeros(qh.shape, F32)
+
+    takes_tails = has_down & (chip == 0)
+
+    @pl.when(takes_tails)
     def _():
         for i in range(2):
             send(6, ht.at[1], tr.at[i], peers[4], 6 + i).wait_recv()
             send(11, ql_ref, qt.at[i], peers[4], 11 + i).wait_recv()
 
-    @pl.when(chip == 1)
+    @pl.when(jnp.logical_not(takes_tails))
     def _():
         tr[...] = jnp.zeros(tr.shape, F32)
         qt[...] = jnp.zeros(qt.shape, F32)
@@ -401,27 +451,24 @@
     out[0:64] = tt[0, pl.ds(pl.multiple_of(64 * core, 8), 64), :F]
     out[64:72] = tt[1, pl.ds(pl.multiple_of(8 * o, 8), 8), :F]
 
-    for c in (to_beside, to_sibling, *(to_prev_segment(i) for i in range(2))):
+    for c in (to_beside, to_sibling, hand_on(1, 4 + far), *swap, *cross, last):
         c.wait_send()
-    for i, there in enumerate((4 + far, o, far, 8 + core)):
-        hand_on(1 + i, there).wait_send()
-
-    @pl.when(core == 0)
+    with_up("wait_send", to_prev_segment(0), to_prev_segment(1), hand_on(4, 8 + core), tails, tail_ql)
+    with_down("wait_send", hand_on(2, o), hand_on(3, far), *heads, *head_ql)
+
+    @pl.when(has_up & (core == 0))
     def _():
         hand_on(5, 10, SHORT).wait_send()
 
-    @pl.when(o < 2)
+    @pl.when(has_down & (o < 2))
     def _():
         for i in range(2):
             to_next_segment(i, TILES).wait_send()
 
-    @pl.when(o == 2)
+    @pl.when(has_down & (o == 2))
     def _():
         for i in range(2):
             to_next_segment(i, SHORT).wait_send()
-
-    for c in (*swap, *cross, *heads, tails, *head_ql, tail_ql, last):
-        c.wait_send()
 
 
 def body(density, operators, owner_count, group_count, target_slot, source_box):

time: 49.6 us -> 39.7 us (0.80)
  the two profiles are of different devices: /device:TPU:1 before, /device:TPU:321 now
where the time goes in v6:
time: 39.7 us; the launch traced here: 39.6 us
  Pallas kernels  38 us (96%)
  local copies, waits for them, and re-layouts  1.55 us (4%)
    pallas_call x1, Pallas kernels, body(): pl.pallas_call(kernel, out_shape=jax.ShapeDtypeStruct((ROWS, F), F32), in...  38 us
    unnamed x1, local copies, waits for them, and re-layouts  1.55 us

profile of v6, /device:TPU:321, one launch (start us, length us, event | category | flops | bytes accessed | tf_op | source)
XLA Modules:
  0.0 39.6 jit_solution(7206272867345219721)
XLA Ops:
  0.0 38.0 %translate.1 = f32[72,296]{1,0:T(8,128)} custom-call(f32[72,296]{1,0:T(8,128)} %den_hbm.1, f32[16,296,296]{2,1,0:T(8,128)} %ops.1, s32[1,128]{1,0:T(1,128)} %bitcast.2, s32[1,128]{1,0:T(1,128)} %bitcast.3, s32[1,16,288]{2,1,0:T(8,128)} %tgt_hbm.1, s32[1,16,288]{2,1,0:T(8,128)} %src_hbm.1), custom_call_target="tpu_custom_call" | custom-call | tf_op jit(solution)/shard_map/translate/pallas_call | solution.py:521
  38.0 1.5 %copy.8 = f32[72,296]{1,0:T(8,128)} copy(f32[72,296]{1,0:T(8,128)} %translate.1) | data formatting | bytes 170496

commit v7 on v6

--- a/solution.py
+++ b/solution.py
@@ -293,21 +293,35 @@
     gather_main(0, False)
     gather_left(0, False)
 
-    @pl.when(has_down)
-    def _():
-        arrived(sib)
-        arrived((sib + 2) % 4)
-
-    @pl.when(has_up)
-    def _():
-        arrived(9 - core)
-
-    @pl.when(has_up & (core == 1))
-    def _():
-        arrived(10, SHORT)
-
-    turn_next()
-    turn_prev()
+    def took_prev():
+        @pl.when(has_down)
+        def _():
+            arrived(sib)
+            arrived((sib + 2) % 4)
+
+        turn_prev()
+
+    def took_next():
+        @pl.when(has_up)
+        def _():
+            arrived(9 - core)
+
+        @pl.when(has_up & (core == 1))
+        def _():
+            arrived(10, SHORT)
+
+        turn_next()
+
+    @pl.when(even)
+    def _():
+        took_next()
+        took_prev()
+
+    @pl.when(odd)
+    def _():
+        took_prev()
+        took_next()
+
     gather_main(1, True)
 
     acc[...] = jnp.zeros(acc.shape, F32)
@@ -355,6 +369,8 @@
     q0 = acc[mine, :128] + ra[:, :128]
     q1 = acc[mine, 128:256] + ra[:, 128:]
     q_ref[0], q_ref[1] = q0, q1
+    cross = [send(2, q_ref.at[1 - chip], rq, beside), send(3, ql_ref, rql, beside)]
+    cross[0].start()
     hi, lo = split(jnp.concatenate([q0, q1], axis=1))
     edges = jnp.dot(hi, hot_send[...], preferred_element_type=F32)
     edges = edges + jnp.dot(lo, hot_send[...], preferred_element_type=F32)
@@ -366,7 +382,6 @@
             )
     heads = [send(4 + i, ht.at[0], hr.at[chip], peers[4 + i], 4 + chip) for i in range(2)]
     tails = send(6, ht.at[1], tr.at[chip], (up, core), 6 + chip)
-    cross = [send(2, q_ref.at[1 - chip], rq, beside), send(3, ql_ref, rql, beside)]
 
     def with_up(name, *copies):
         for c in copies:
@@ -379,7 +394,6 @@
     with_down("start", heads[1])
     with_up("start", tails)
     with_down("start", heads[0])
-    cross[0].start()
     lax.fori_loop(0, 2, multiply_side, 0)
     u = side[...]
     u = u + pltpu.roll(u, 64, 1)

time: 39.7 us -> 39.8 us (level)
  the two profiles are of different devices: /device:TPU:321 before, /device:TPU:385 now
where the time goes in v7:
time: 39.8 us; the launch traced here: 39.7 us
  Pallas kernels  38.1 us (96%)
  local copies, waits for them, and re-layouts  1.55 us (4%)
    pallas_call x1, Pallas kernels, body(): pl.pallas_call(kernel, out_shape=jax.ShapeDtypeStruct((ROWS, F), F32), in...  38.1 us
    unnamed x1, local copies, waits for them, and re-layouts  1.55 us

profile of v7, /device:TPU:385, one launch (start us, length us, event | category | flops | bytes accessed | tf_op | source)
XLA Modules:
  0.0 39.7 jit_solution(4666613595023729086)
XLA Ops:
  0.0 38.1 %translate.1 = f32[72,296]{1,0:T(8,128)} custom-call(f32[72,296]{1,0:T(8,128)} %den_hbm.1, f32[16,296,296]{2,1,0:T(8,128)} %ops.1, s32[1,128]{1,0:T(1,128)} %bitcast.2, s32[1,128]{1,0:T(1,128)} %bitcast.3, s32[1,16,288]{2,1,0:T(8,128)} %tgt_hbm.1, s32[1,16,288]{2,1,0:T(8,128)} %src_hbm.1), custom_call_target="tpu_custom_call" | custom-call | tf_op jit(solution)/shard_map/translate/pallas_call | solution.py:535
  38.1 1.5 %copy.8 = f32[72,296]{1,0:T(8,128)} copy(f32[72,296]{1,0:T(8,128)} %translate.1) | data formatting | bytes 170496

commit v8 on v7

--- a/solution.py
+++ b/solution.py
@@ -72,8 +72,6 @@
     inputs = [pltpu.make_async_copy(a, v, in_sem.at[i]) for i, (a, v) in enumerate(pairs)]
     for c in inputs:
         c.start()
-    for k in range(OFFS):
-        op_copy(k).start()
     inputs[0].wait()
 
     me = 4 + o
@@ -83,6 +81,41 @@
     for rt in range(9):
         for h in range(2):
             rx[me, 3 + 2 * rt + h] = den[8 * rt : 8 * rt + 8, 128 * h : 128 * h + 128]
+
+    def block_copy(here, there, count, send, device):
+        return pltpu.make_async_remote_copy(
+            src_ref=rx.at[here, pl.ds(0, count)], dst_ref=rx.at[there, pl.ds(0, count)],
+            send_sem=send, recv_sem=rsem.at[there], device_id=device, device_id_type=MESH,
+        )
+
+    pl.semaphore_wait(barrier, jnp.where(has_up & has_down, 6, 4))
+
+    def to_prev_segment(i):
+        return block_copy(me, o, TILES, ici_send.at[1 + i], peers[2 + i])
+
+    def to_next_segment(i, count):
+        return block_copy(me, 8 + o, count, ici_send.at[3 + i], peers[4 + i])
+
+    to_beside = block_copy(me, me, TILES, ici_send.at[0], beside)
+    to_sibling = block_copy(me, me, TILES, sib_send.at[0], sibling)
+    for i in (1, 0):
+
+        @pl.when(has_up)
+        def _():
+            to_prev_segment(i).start()
+
+        @pl.when(has_down & (o < 2))
+        def _():
+            to_next_segment(i, TILES).start()
+
+        @pl.when(has_down & (o == 2))
+        def _():
+            to_next_segment(i, SHORT).start()
+
+    to_beside.start()
+    to_sibling.start()
+    for k in range(OFFS):
+        op_copy(k).start()
 
     for c in inputs[1:]:
         c.wait()
@@ -131,38 +164,6 @@
     hot_recv[:, :128] = jnp.where(slot == slot_of_column(lane + 128 * chip), 1.0, 0.0).astype(BF16)
     hot_recv[:, 128:] = jnp.where((lane < 32) & (slot == slot_of_column(lane + 256)), 1.0, 0.0).astype(BF16)
 
-    def block_copy(here, there, count, send, device):
-        return pltpu.make_async_remote_copy(
-            src_ref=rx.at[here, pl.ds(0, count)], dst_ref=rx.at[there, pl.ds(0, count)],
-            send_sem=send, recv_sem=rsem.at[there], device_id=device, device_id_type=MESH,
-        )
-
-    pl.semaphore_wait(barrier, jnp.where(has_up & has_down, 6, 4))
-
-    def to_prev_segment(i):
-        return block_copy(me, o, TILES, ici_send.at[1 + i], peers[2 + i])
-
-    def to_next_segment(i, count):
-        return block_copy(me, 8 + o, count, ici_send.at[3 + i], peers[4 + i])
-
-    to_beside = block_copy(me, me, TILES, ici_send.at[0], beside)
-    to_sibling = block_copy(me, me, TILES, sib_send.at[0], sibling)
-    for i in (1, 0):
-
-        @pl.when(has_up)
-        def _():
-            to_prev_segment(i).start()
-
-        @pl.when(has_down & (o < 2))
-        def _():
-            to_next_segment(i, TILES).start()
-
-        @pl.when(has_down & (o == 2))
-        def _():
-            to_next_segment(i, SHORT).start()
-
-    to_beside.start()
-    to_sibling.start()
 
     stage[:, pl.ds(F, 8), :] = jnp.zeros((OFFS, 8, F), F32)
 

time: 39.8 us -> 38.4 us (0.965)
  the two profiles are of different devices: /device:TPU:385 before, /device:TPU:321 now
where the time goes in v8:
time: 38.4 us; the launch traced here: 38.2 us
  Pallas kernels  36.7 us (96%)
  local copies, waits for them, and re-layouts  1.55 us (4%)
    pallas_call x1, Pallas kernels, body(): pl.pallas_call(kernel, out_shape=jax.ShapeDtypeStruct((ROWS, F), F32), in...  36.7 us
    unnamed x1, local copies, waits for them, and re-layouts  1.55 us

profile of v8, /device:TPU:321, one launch (start us, length us, event | category | flops | bytes accessed | tf_op | source)
XLA Modules:
  0.0 38.2 jit_solution(17248046233111602667)
XLA Ops:
  0.0 36.7 %translate.1 = f32[72,296]{1,0:T(8,128)} custom-call(f32[72,296]{1,0:T(8,128)} %den_hbm.1, f32[16,296,296]{2,1,0:T(8,128)} %ops.1, s32[1,128]{1,0:T(1,128)} %bitcast.2, s32[1,128]{1,0:T(1,128)} %bitcast.3, s32[1,16,288]{2,1,0:T(8,128)} %tgt_hbm.1, s32[1,16,288]{2,1,0:T(8,128)} %src_hbm.1), custom_call_target="tpu_custom_call" | custom-call | tf_op jit(solution)/shard_map/translate/pallas_call | solution.py:536
  36.7 1.5 %copy.8 = f32[72,296]{1,0:T(8,128)} copy(f32[72,296]{1,0:T(8,128)} %translate.1) | data formatting | bytes 170496
